TPU v7x, 128 devices: a whole 4x4x4 slice. The times are simulated.
128 devices in a mesh: band: 32 (over y, x_lo, z), col: 4 (over x_hi, core).
Axes of the slice: x: 4 (x_hi: 2, x_lo: 2; x = x_hi * 2 + x_lo), y: 4, z: 4, core: 2. Of those that a mesh axis runs over, the one named last changes fastest.
Arguments:
- demand: float32 [131072, 16], P(('band', 'col')), may hold values from -16 to 16
- lead_periods: int32 [131072], P(('band', 'col')), may hold values from 1 to 4
- matrix_tiles: float32 [32, 4, 128, 128, 128], P('band', 'col'), may hold values from -0.125 to 0.125
- tile_pos: int32 [32, 4, 128], P('band', 'col'), may hold values from 0 to 8191, as said below
- cost_vector: float32 [131072], P(('band', 'col')), may hold values from 0.05 to 7
- primal_init: float32 [131072, 16], P(('band', 'col')), may hold values from 0 to 2
- dual_init: float32 [131072, 16], P(('band', 'col')), may hold values from -6 to 6
- weight_init: float32 [16], replicated, may hold values from 0.5 to 2
Outputs:
- primal: float32 [131072, 16], P(('band', 'col'))
- dual_vars: float32 [131072, 16], P(('band', 'col'))
- weight: float32 [16], replicated
Inputs may be any that keep to these rules, and one draw needn't show every extreme that they name: `tile_pos`: within one period and column block the 128 entries are different; entry v places its tile at row tile v // 256 of that period and column tile v % (256) of that column block.
All inputs are finite; a program needn't handle non-finite values.
Results may differ from a plain program's by a relative error of at most 0.0003.
Values sent between devices are 32-bit elements; how exact they have to be, the bound alone decides.
A program may use at most 64 MiB of HBM per device.

v0:
```python
import jax
import jax.numpy as jnp
from jax import lax
from jax.sharding import PartitionSpec as P

ITERS = 3
LEAD_MAX = 4


step_scale = 0.45
return_share = 0.6
epsilon = 1e-06
highest = lax.Precision.HIGHEST


def passed_along(value, axis, steps):
    count = lax.axis_size(axis)
    pairs = [(source, (source + steps) % count) for source in range(count)]
    return lax.ppermute(value, axis, pairs)


def forward_part(matrix_tiles, positions, column_block, units_col, units_row):
    tile_size = matrix_tiles.shape[-1]
    scen_count = column_block.shape[-1]
    blocks = column_block.reshape(-1, tile_size, scen_count)
    picked = blocks[positions % units_col]
    product = jnp.einsum("tij,tjs->tis", matrix_tiles, picked, precision=highest)
    onehot = (
        positions[None, :] // units_col == jnp.arange(units_row, dtype=jnp.int32)[:, None]
    ).astype(jnp.float32)
    result = jnp.dot(onehot, product.reshape(product.shape[0], -1), precision=highest)
    return result.reshape(units_row * tile_size, scen_count)


def backward_part(matrix_tiles, positions, band_dual, units_col):
    tile_size = matrix_tiles.shape[-1]
    scen_count = band_dual.shape[-1]
    blocks = band_dual.reshape(-1, tile_size, scen_count)
    picked = blocks[positions // units_col]
    product = jnp.einsum("tij,tis->tjs", matrix_tiles, picked, precision=highest)
    result = jax.ops.segment_sum(product, positions % units_col, num_segments=units_col)
    return result.reshape(units_col * tile_size, scen_count)


def on_device(
    demand, lead_periods, matrix_tiles, tile_pos, cost_vector, primal_init, dual_init, weight_init
):
    band_count = lax.axis_size("band")
    column_count = lax.axis_size("col")
    matrix_tiles = matrix_tiles.reshape(matrix_tiles.shape[2:])
    positions = tile_pos.reshape(-1)
    tile_size = matrix_tiles.shape[-1]
    block_rows = demand.shape[0]
    sub_count = block_rows // tile_size
    units_col = band_count * sub_count
    units_row = column_count * sub_count
    earlier = demand
    lagged = jnp.zeros_like(demand)
    for lead in range(1, LEAD_MAX + 1):
        earlier = passed_along(earlier, "band", 1)
        lagged = jnp.where(lead_periods[:, None] == lead, earlier, lagged)
    right_side = demand - return_share * lagged
    primal = primal_init
    dual_vars = dual_init
    weight = weight_init
    for iteration in range(ITERS):
        primal_step = (step_scale / weight)[None, :]
        dual_step = (step_scale * weight)[None, :]
        band_dual = lax.all_gather(dual_vars, "col", axis=0, tiled=True)
        partial_value = backward_part(matrix_tiles, positions, band_dual, units_col)
        pull_terms = lax.psum_scatter(partial_value, "band", scatter_dimension=0, tiled=True)
        primal_new = jnp.maximum(primal - primal_step * (cost_vector[:, None] - pull_terms), 0.0)
        primal_change = primal_new - primal
        column_block = lax.all_gather(2.0 * primal_new - primal, "band", axis=0, tiled=True)
        primal_local = jnp.sum(primal_change * primal_change, axis=0)
        primal_square = lax.psum(primal_local, ("band", "col"))
        push_part = forward_part(matrix_tiles, positions, column_block, units_col, units_row)
        push_terms = lax.psum_scatter(push_part, "col", scatter_dimension=0, tiled=True)
        dual_new = dual_vars + dual_step * (right_side - push_terms)
        dual_change = dual_new - dual_vars
        dual_local = jnp.sum(dual_change * dual_change, axis=0)
        dual_square = lax.psum(dual_local, ("band", "col"))
        weight = jnp.sqrt(weight * jnp.sqrt((primal_square + epsilon) / (dual_square + epsilon)))
        primal = primal_new
        dual_vars = dual_new
    return (primal, dual_vars, weight)


def solution(mesh):
    in_specs = (
        P(("band", "col"), None),
        P(("band", "col")),
        P("band", "col", None, None, None),
        P("band", "col", None),
        P(("band", "col")),
        P(("band", "col"), None),
        P(("band", "col"), None),
        P(),
    )
    out_specs = (P(("band", "col"), None), P(("band", "col"), None), P())
    return jax.shard_map(
        on_device, mesh=mesh, in_specs=in_specs, out_specs=out_specs, check_vma=False
    )
```

profile of v0, /device:TPU:1, one launch (start us, length us, event | category | flops | bytes accessed | tf_op | source)
XLA Modules:
  0.0 1255.0 jit_solution(2202049545726757374)
XLA Ops:
  8.6 8.8 all_gather.18
  18.2 9.5 fusion.12
  27.8 5.2 scatter_fusion
  35.1 140.7 %reduce-scatter.7.cloned.1.call-done = f32[1024,16]{0,1:T(8,128)} async-done(((f32[32768,16]{0,1:T(8,128)}), f32[1024,16]{0,1:T(8,128)}) %reduce-scatter.7.cloned.1.call-update) | async-done | bytes 65552 | tf_op jit(solution)/shard_map/reduce_scatter | solution.py:71
  177.7 153.2 %all-gather.4.cloned.1.call-done = f32[32768,16]{0,1:T(8,128)} async-done(((f32[1024,16]{0,1:T(8,128)}), f32[32768,16]{0,1:T(8,128)}) %all-gather.4.cloned.1.call-update) | async-done | bytes 2097168 | tf_op jit(solution)/shard_map/all_gather | solution.py:74
  330.9 1.7 copy_bitcast_fusion.5
  333.4 15.4 %fusion.15 = f32[128,128,16]{1,2,0:T(8,128)S(1)} fusion(f32[128,128,16]{1,2,0:T(8,128)S(1)} %gather_fusion.1, f32[1,1,128,128,128]{4,3,2,1,0:T(8,128)} %param.10), kind=kOutput, calls=%fused_computation.28 | convolution fusion | flops 402653184 | bytes 10485760 | tf_op jit(solution)/shard_map/tij,tjs->tis/dot_general | solution.py:27
  353.5 6.2 collective-permute-done
  359.7 7.3 collective-permute-done.1
  367.1 7.3 collective-permute-done.2
  374.4 7.7 collective-permute-done.3
  382.1 17.7 %reduce-scatter.9.cloned.1.call-done = f32[1024,16]{0,1:T(8,128)} async-done(((f32[4096,16]{0,1:T(8,128)}), f32[1024,16]{0,1:T(8,128)}) %reduce-scatter.9.cloned.1.call-update) | async-done | bytes 65552 | tf_op jit(solution)/shard_map/reduce_scatter | solution.py:78
  400.8 15.5 %all_gather.20 = f32[4096,16]{0,1:T(8,128)S(1)} all-gather(f32[1024,16]{0,1:T(8,128)S(1)} %get-tuple-element.24), channel_id=1, replica_groups=mesh['band'=32,'col'=4] {'col'}, dimensions={0}, use_global_device_ids=true | all-gather | bytes 327680 | tf_op jit(solution)/shard_map/all_gather | solution.py:69
  417.1 9.5 fusion.18
  426.7 5.2 scatter_fusion.1
  433.5 63.4 %all-reduce.2 = (f32[16]{0:T(128)S(1)}, f32[16]{0:T(128)S(1)}) all-reduce(f32[16]{0:T(128)S(1)} %get-tuple-element.23, f32[16]{0:T(128)S(1)} %get-tuple-element.21), channel_id=1, replica_groups=mesh['band'=32,'col'=4] {'band','col'}, use_global_device_ids=true, to_apply=%region_6.7 | all-reduce | flops 32 | bytes 256 | tf_op jit(solution)/shard_map/psum | solution.py:82
  496.9 71.5 %reduce-scatter.11.cloned.1.call-done = f32[1024,16]{0,1:T(8,128)} async-done(((f32[32768,16]{0,1:T(8,128)}), f32[1024,16]{0,1:T(8,128)}) %reduce-scatter.11.cloned.1.call-update) | async-done | bytes 65552 | tf_op jit(solution)/shard_map/reduce_scatter | solution.py:71
  570.4 152.9 %all-gather.6.cloned.1.call-done = f32[32768,16]{0,1:T(8,128)} async-done(((f32[1024,16]{0,1:T(8,128)}), f32[32768,16]{0,1:T(8,128)}) %all-gather.6.cloned.1.call-update) | async-done | bytes 2097168 | tf_op jit(solution)/shard_map/all_gather | solution.py:74
  723.3 1.7 copy_bitcast_fusion.4
  725.8 15.4 %fusion.21 = f32[128,128,16]{1,2,0:T(8,128)S(1)} fusion(f32[128,128,16]{1,2,0:T(8,128)S(1)} %gather_fusion.3, f32[1,1,128,128,128]{4,3,2,1,0:T(8,128)} %param.10), kind=kOutput, calls=%fused_computation.30 | convolution fusion | flops 402653184 | bytes 10485760 | tf_op jit(solution)/shard_map/tij,tjs->tis/dot_general | solution.py:27
  744.6 47.4 %reduce-scatter.13.cloned.1.call-done = f32[1024,16]{0,1:T(8,128)} async-done(((f32[4096,16]{0,1:T(8,128)}), f32[1024,16]{0,1:T(8,128)}) %reduce-scatter.13.cloned.1.call-update) | async-done | bytes 65552 | tf_op jit(solution)/shard_map/reduce_scatter | solution.py:78
  793.1 8.3 all_gather.22
  802.2 9.5 fusion.24
  811.8 5.2 scatter_fusion.2
  818.6 65.7 %all-reduce.1 = (f32[16]{0:T(128)S(1)}, f32[16]{0:T(128)S(1)}) all-reduce(f32[16]{0:T(128)S(1)} %get-tuple-element.17, f32[16]{0:T(128)S(1)} %get-tuple-element.15), channel_id=1, replica_groups=mesh['band'=32,'col'=4] {'band','col'}, use_global_device_ids=true, to_apply=%region_13.14 | all-reduce | flops 32 | bytes 256 | tf_op jit(solution)/shard_map/psum | solution.py:82
  884.3 73.3 %reduce-scatter.15.cloned.1.call-done = f32[1024,16]{0,1:T(8,128)} async-done(((f32[32768,16]{0,1:T(8,128)}), f32[1024,16]{0,1:T(8,128)}) %reduce-scatter.15.cloned.1.call-update) | async-done | bytes 65552 | tf_op jit(solution)/shard_map/reduce_scatter | solution.py:71
  959.5 152.7 %all-gather.8.cloned.1.call-done = f32[32768,16]{0,1:T(8,128)} async-done(((f32[1024,16]{0,1:T(8,128)}), f32[32768,16]{0,1:T(8,128)}) %all-gather.8.cloned.1.call-update) | async-done | bytes 2097168 | tf_op jit(solution)/shard_map/all_gather | solution.py:74
  1112.2 1.7 copy_bitcast_fusion.3
  1114.7 15.4 %fusion.27 = f32[128,128,16]{1,2,0:T(8,128)S(1)} fusion(f32[128,128,16]{1,2,0:T(8,128)S(1)} %gather_fusion.5, f32[1,1,128,128,128]{4,3,2,1,0:T(8,128)} %param.10), kind=kOutput, calls=%fused_computation.32 | convolution fusion | flops 402653184 | bytes 10485760 | tf_op jit(solution)/shard_map/tij,tjs->tis/dot_general | solution.py:27
  1133.5 47.5 %reduce-scatter.17.cloned.1.call-done = f32[1024,16]{0,1:T(8,128)} async-done(((f32[4096,16]{0,1:T(8,128)}), f32[1024,16]{0,1:T(8,128)}) %reduce-scatter.17.cloned.1.call-update) | async-done | bytes 65552 | tf_op jit(solution)/shard_map/reduce_scatter | solution.py:78
  1181.0 1.7 multiply_reduce_fusion
  1182.6 65.1 %all-reduce = (f32[16]{0:T(128)S(1)}, f32[16]{0:T(128)S(1)}) all-reduce(f32[16]{0:T(128)S(1)} %get-tuple-element.11, f32[16]{0:T(128)S(1)} %get-tuple-element.9), channel_id=1, replica_groups=mesh['band'=32,'col'=4] {'band','col'}, use_global_device_ids=true, to_apply=%region_20.21 | all-reduce | flops 32 | bytes 256 | tf_op jit(solution)/shard_map/psum | solution.py:82
  (85 shorter events, 31.6 us)
Async XLA Ops:
  7.2 168.6 %reduce-scatter.7.cloned.1.call-start = ((), (), s32[]{:S(2)}) async-start(), calls=%async_computation.6 | async-start | bytes 2162688 | tf_op jit(solution)/shard_map/reduce_scatter | solution.py:71
  34.4 0.7 copy-start.6
  34.4 141.3 %copy-start = (f32[1024,16]{0,1:T(8,128)S(1)}, f32[1024,16]{0,1:T(8,128)}, u32[]{:S(2)}) copy-start(f32[1024,16]{0,1:T(8,128)} %param.13) | copy-start | bytes 196612
  34.5 141.3 %copy-start.4 = (f32[1024]{0:T(1024)S(1)}, f32[1024]{0:T(1024)}, u32[]{:S(2)}) copy-start(f32[1024]{0:T(1024)} %param.12) | copy-start | bytes 12292
  34.5 143.3 %copy-start.7 = (s32[1,1,128]{2,1,0:T(1,128)S(1)}, s32[1,1,128]{2,1,0:T(1,128)}, u32[]{:S(2)}) copy-start(s32[1,1,128]{2,1,0:T(1,128)} %param.11) | copy-start | bytes 1540
  34.5 296.4 %all-gather.4.cloned.1.call-start = ((), (), s32[]{:S(2)}) async-start(), calls=%async_computation.7 | async-start | bytes 2162688 | tf_op jit(solution)/shard_map/all_gather | solution.py:74
  177.5 222.3 %reduce-scatter.9.cloned.1.call-start = ((), (), s32[]{:S(2)}) async-start(), calls=%async_computation.8 | async-start | bytes 327680 | tf_op jit(solution)/shard_map/reduce_scatter | solution.py:78
  350.2 2.1 copy-start.3
  350.2 24.2 %copy-start.5 = (s32[1024]{0:T(1024)S(1)}, s32[1024]{0:T(1024)}, u32[]{:S(2)}) copy-start(s32[1024]{0:T(1024)} %param.9) | copy-start | bytes 12292
  350.2 49.5 %copy-start.1 = (f32[1024,16]{0,1:T(8,128)S(1)}, f32[1024,16]{0,1:T(8,128)}, u32[]{:S(2)}) copy-start(f32[1024,16]{0,1:T(8,128)} %param.14) | copy-start | bytes 196612
  352.3 216.1 %reduce-scatter.11.cloned.1.call-start = ((), (), s32[]{:S(2)}) async-start(), calls=%async_computation.9 | async-start | bytes 2162688 | tf_op jit(solution)/shard_map/reduce_scatter | solution.py:71
  352.3 7.4 collective-permute-start
  359.7 7.3 collective-permute-start.1
  367.1 7.3 collective-permute-start.2
  374.4 7.7 collective-permute-start.3
  433.4 289.9 %all-gather.6.cloned.1.call-start = ((), (), s32[]{:S(2)}) async-start(), calls=%async_computation.10 | async-start | bytes 2162688 | tf_op jit(solution)/shard_map/all_gather | solution.py:74
  570.1 222.0 %reduce-scatter.13.cloned.1.call-start = ((), (), s32[]{:S(2)}) async-start(), calls=%async_computation.11 | async-start | bytes 327680 | tf_op jit(solution)/shard_map/reduce_scatter | solution.py:78
  744.6 212.9 %reduce-scatter.15.cloned.1.call-start = ((), (), s32[]{:S(2)}) async-start(), calls=%async_computation.12 | async-start | bytes 2162688 | tf_op jit(solution)/shard_map/reduce_scatter | solution.py:71
  818.5 293.6 %all-gather.8.cloned.1.call-start = ((), (), s32[]{:S(2)}) async-start(), calls=%async_computation.13 | async-start | bytes 2162688 | tf_op jit(solution)/shard_map/all_gather | solution.py:74
  958.6 155.4 %copy-start.2 = (f32[1024,16]{0,1:T(8,128)}, f32[1024,16]{0,1:T(8,128)S(1)}, u32[]{:S(2)}) copy-start(f32[1024,16]{0,1:T(8,128)S(1)} %get-tuple-element.10) | copy-start | bytes 196612
  959.2 221.7 %reduce-scatter.17.cloned.1.call-start = ((), (), s32[]{:S(2)}) async-start(), calls=%async_computation.14 | async-start | bytes 327680 | tf_op jit(solution)/shard_map/reduce_scatter | solution.py:78
Sparse Core Ops, SparseCore 0:
  34.6 141.1 reduce-scatter.6
  178.1 152.7 all-gather.3
  352.4 47.3 reduce-scatter.8
  433.5 134.8 reduce-scatter.10
  570.6 152.6 all-gather.5
  744.7 47.3 reduce-scatter.12
  818.7 138.8 reduce-scatter.14
  959.8 152.2 all-gather.7
  1133.6 47.3 reduce-scatter.16
where the time goes:
time: 1260 us; the launch traced here: 1250 us
  waiting for transfers between devices  885 us (70%)
  blocking collectives  227 us (18%)
  matrix products  76.5 us (6%)
  other arithmetic  26.2 us (2%)
  local copies, waits for them, and re-layouts  23.4 us (2%)
  between operations  14.4 us (1%)
    all_gather x3, waiting for transfers between devices, on_device(): lax.all_gather(2.0 * primal_new - primal, 'band', axis=0, tiled=True)  459 us
    reduce_scatter x3, waiting for transfers between devices, on_device(): lax.psum_scatter(partial_value, 'band', scatter_dimension=0, tiled=True)  285 us
    psum x3, blocking collectives, on_device(): dual_square = lax.psum(dual_local, ('band', 'col'))  194 us
    reduce_scatter x3, waiting for transfers between devices, on_device(): lax.psum_scatter(push_part, 'col', scatter_dimension=0, tiled=True)  113 us
    dot_general x3, matrix products, forward_part(): jnp.einsum('tij,tjs->tis', matrix_tiles, picked, precision=highest)  46.1 us
    all_gather x3, blocking collectives, on_device(): band_dual = lax.all_gather(dual_vars, 'col', axis=0, tiled=True)  32.7 us
    ppermute x4, waiting for transfers between devices, passed_along(): return lax.ppermute(value, axis, pairs)  28.5 us
    dot_general x3, matrix products, backward_part(): jnp.einsum('tij,tis->tjs', matrix_tiles, picked, precision=highest)  28.4 us
  transfers between devices with their start and end apart: 13, of which 13 were waited for; matrix products, arithmetic and copies ran while one was open for 0% of the time, Pallas kernels for 0%

commit v1 on v0

v1 whole, which is shorter than its diff:
```python
import jax
import jax.numpy as jnp
from jax import lax
from jax.experimental import pallas as pl
from jax.experimental.pallas import tpu as pltpu
from jax.sharding import PartitionSpec as P

ITERS = 3
LEAD_MAX = 4
step_scale = 0.45
return_share = 0.6
epsilon = 1e-06

NT = 128
T = 128
CT = 256
RT = 32
F32 = jnp.float32
BF16 = jnp.bfloat16
CHUNKS = 16
MESH = pl.DeviceIdType.MESH

O_ROW, O_C0, O_C1, O_PC, O_PR = 0, 128, 256, 384, 512
O_L0, O_L1, O_LR = 640, 896, 1152
TABLE = 1184


def index_table(pos):
    pos = pos.reshape(-1)
    t = jnp.arange(NT, dtype=jnp.int32)
    row, col = pos // CT, pos % CT

    def order(c):
        k, z, x, y = c % 8, (c // 8) % 4, (c // 32) % 2, c // 64
        return ((z * 4 + y) * 2 + x) * 8 + k, ((y * 4 + z) * 2 + x) * 8 + k

    def prev(key):
        same = (key[:, None] == key[None, :]) & (t[:, None] < t[None, :])
        found = jnp.max(jnp.where(same, t[:, None], -1), axis=0)
        return jnp.where(found < 0, NT, found)

    def last(key, count):
        ids = jnp.arange(count, dtype=jnp.int32)
        found = jnp.max(jnp.where(key[:, None] == ids[None, :], t[:, None], -1), axis=0)
        return jnp.where(found < 0, NT, found)

    c0, c1 = order(col)
    drow = (row // 8) * 10 + row % 8
    return jnp.concatenate(
        [drow, c0, c1, prev(col), prev(row), last(c0, CT), last(c1, CT), last(row, RT)]
    )


def split(v):
    hi = v.astype(BF16).astype(F32)
    return hi, v - hi


class Copies:
    def __init__(self, make, count):
        self.make, self.count = make, count

    def __getitem__(self, i):
        return self.make(i)


def kernel(
    tab, dem, lead, a_hbm, cost, prim0, dual0, w0,
    prim_out, dual_out, w_out,
    af, wt, s_buf, xg0, xg1, pb, fb, rb, qb, tb, dg0, dg1, yb, cr, pr, rhs, lag, wgt, fs, fc, fz, fp,
    a_sem, lag_s, lag_r, ca_s, ca_r, rz_s, rz_r, rp_s, rp_r, ap_s, ap_r, az_s, az_r, cs_s, cs_r, fi_s, fi_r,
):
    b = lax.axis_index("band")
    q = lax.axis_index("col")
    y, x, z = b // 8, (b // 4) % 2, b % 4

    def rc(src, dst, ss, rs, band, col):
        return pltpu.make_async_remote_copy(
            src_ref=src, dst_ref=dst, send_sem=ss, recv_sem=rs,
            device_id=(band, col), device_id_type=MESH,
        )

    xg, dg = (xg0, xg1), (dg0, dg1)

    g_of = (z, y)
    m_of = (y * 2 + x, z * 2 + x)

    def band_of(h, g, m):
        o, xx = m // 2, m % 2
        return o * 8 + xx * 4 + g if h == 0 else g * 8 + xx * 4 + o

    def a_copy(i):
        n = NT // CHUNKS
        return pltpu.make_async_copy(a_hbm.at[pl.ds(i * n, n)], af.at[pl.ds(i * n, n)], a_sem.at[i])

    def lag_copy(l):
        return rc(dem, lag.at[l - 1], lag_s.at[l - 1], lag_r.at[l - 1], (b + l) % 32, q)

    def ca_copy(h, j):
        own = dg[h].at[pl.ds(q * 10, 10)]
        return rc(own, own, ca_s.at[h, j - 1], ca_r.at[h, j - 1], b, (q + j) % 4)

    def ca_recv(h, j):
        slot = dg[h].at[pl.ds(((q + 4 - j) % 4) * 10, 10)]
        return rc(slot, slot, ca_s.at[h, j - 1], ca_r.at[h, j - 1], b, (q + 4 - j) % 4)

    def ring(h):
        g = g_of[h]
        return g, (g + 1) % 4, (g + 3) % 4, (g + 2) % 4

    def rz_copies(h):
        g, up, dn, opp = ring(h)
        m = m_of[h]
        bu, bd = band_of(h, up, m), band_of(h, dn, m)

        def piece(block, half):
            return pb.at[h, pl.ds(block * 66 + (34 if half else 0), 32 if half else 34)]

        spec = (
            (piece(opp, 0), fb.at[h, 0], bu),
            (piece(opp, 1), fb.at[h, 1, pl.ds(0, 32)], bd),
            (piece(up, 1), rb.at[h, 0, pl.ds(34, 32)], bu),
            (piece(dn, 0), rb.at[h, 1, pl.ds(0, 34)], bd),
            (piece(up, 0), rb.at[h, 0, pl.ds(0, 34)], bu),
            (piece(dn, 1), rb.at[h, 1, pl.ds(34, 32)], bd),
        )
        return Copies(
            lambda i: rc(spec[i][0], spec[i][1], rz_s.at[h, i], rz_r.at[h, i], spec[i][2], q), 6
        )

    def rp_copy(h, j):
        m2 = (m_of[h] + j) % 8
        return rc(
            qb.at[h, m2], tb.at[h, j - 1], rp_s.at[h, j - 1], rp_r.at[h, j - 1], band_of(h, g_of[h], m2), q
        )

    def ap_copy(h, j, back=False):
        m = m_of[h]
        m2 = (m + 8 - j) % 8 if back else (m + j) % 8
        slot = xg[h].at[pl.ds((g_of[h] * 8 + (m2 if back else m)) * 8, 8)]
        return rc(slot, slot, ap_s.at[h, j - 1], ap_r.at[h, j - 1], band_of(h, g_of[h], m2), q)

    def az_copies(h, back=False):
        g, up, dn, opp = ring(h)
        m = m_of[h]
        bu, bd = band_of(h, up, m), band_of(h, dn, m)

        def piece(block, half):
            return xg[h].at[pl.ds(block * 64 + half * 32, 32)]

        lo, hi = (dn, up) if back else (g, g)
        spec = (
            (piece(lo, 0), bu),
            (piece(hi, 1), bd),
            (piece(lo, 1), bu),
            (piece(hi, 0), bd),
            (piece(opp if back else dn, 0), bu),
            (piece(opp if back else up, 1), bd),
        )
        return Copies(
            lambda i: rc(spec[i][0], spec[i][0], az_s.at[h, i], az_r.at[h, i], spec[i][1], q), 6
        )

    def cs_copy(h, j):
        q2 = (q + j) % 4
        return rc(yb.at[h, pl.ds(q2 * 8, 8)], cr.at[h, j - 1], cs_s.at[h, j - 1], cs_r.at[h, j - 1], b, q2)

    for i in range(CHUNKS):
        a_copy(i).start()
    zero = jnp.zeros((8, T), F32)
    for h in range(2):
        for k in range(8):
            dg[h][q * 10 + k] = dual0[8 * h:8 * h + 8, k * T:(k + 1) * T]
            pr[h, k] = prim0[8 * h:8 * h + 8, k * T:(k + 1) * T]
        dg[h][q * 10 + 8] = zero
        dg[h][q * 10 + 9] = zero
        wgt[h] = w0[8 * h:8 * h + 8, :]
        for j in (2, 1, 3):
            ca_copy(h, j).start()
    for l in range(1, LEAD_MAX + 1):
        lag_copy(l).start()
    s_buf[NT] = zero

    for i in range(CHUNKS):
        a_copy(i).wait()
        n = NT // CHUNKS

        def prep(t, carry):
            v = af[t]
            hi = v.astype(BF16)
            wt[t, 0] = hi
            wt[t, 1] = (v - hi.astype(F32)).astype(BF16)
            return carry

        lax.fori_loop(i * n, (i + 1) * n, prep, 0, unroll=2)

    def products(h, src, o_src, o_prev, forward):
        def pair(p, carry):
            t1, t2 = 2 * p, 2 * p + 1
            v1 = src[h][tab[o_src + t1]]
            v2 = src[h][tab[o_src + t2]]
            lhs = jnp.concatenate([*split(v1), *split(v2)], axis=0).astype(BF16)
            lhs = jnp.concatenate([lhs, lhs], axis=1)
            h1, l1, h2, l2 = wt[t1, 0], wt[t1, 1], wt[t2, 0], wt[t2, 1]
            if forward:
                w = jnp.concatenate(
                    [jnp.concatenate([h1, l1], axis=1), jnp.concatenate([h2, l2], axis=1)], axis=0
                )
                dims = (((1,), (1,)), ((), ()))
            else:
                w = jnp.concatenate(
                    [jnp.concatenate([h1, h2], axis=1), jnp.concatenate([l1, l2], axis=1)], axis=0
                )
                dims = (((1,), (0,)), ((), ()))
            out = lax.dot_general(lhs, w, dims, preferred_element_type=F32)
            s_buf[t1] = out[0:8, :T] + out[8:16, :T] + s_buf[tab[o_prev + t1]]
            s_buf[t2] = out[16:24, T:] + out[24:32, T:] + s_buf[tab[o_prev + t2]]
            return carry

        lax.fori_loop(0, NT // 2, pair, 0, unroll=4)

    def iteration(it, carry):
        for h in range(2):
            for j in range(1, 4):
                ca_recv(h, j).wait_recv()
            products(h, dg, O_ROW, O_PC, False)
            stat = [sum(dg[h][c * 10 + 8 + e] for c in range(4)) for e in range(2)]
            for g in range(4):
                pb[h, g * 66] = stat[0]
                pb[h, g * 66 + 1] = stat[1]

                def place(i, carry, g=g):
                    pb[h, g * 66 + 2 + i] = s_buf[tab[(O_L0, O_L1)[h] + g * 64 + i]]
                    return carry

                lax.fori_loop(0, 64, place, 0, unroll=8)
            copies = rz_copies(h)
            for i in range(4):
                copies[i].start()
        for h in range(2):
            g, up, dn, opp = ring(h)
            copies = rz_copies(h)
            copies[0].wait_recv()
            here = pl.ds(up * 66, 34)
            pb[h, here] = pb[h, here] + fb[h, 0]
            copies[4].start()
            copies[1].wait_recv()
            here = pl.ds(dn * 66 + 34, 32)
            pb[h, here] = pb[h, here] + fb[h, 1, 0:32]
            copies[5].start()
        for h in range(2):
            g = g_of[h]
            copies = rz_copies(h)
            for i in (2, 3, 4, 5):
                copies[i].wait_recv()
            stat = [pb[h, g * 66 + e] + rb[h, 0, e] + rb[h, 1, e] for e in range(2)]
            for m in range(8):
                for k in range(8):
                    i = 2 + m * 8 + k
                    qb[h, m, k] = pb[h, g * 66 + i] + rb[h, 0, i] + rb[h, 1, i]
                for e in range(2):
                    qb[h, m, 8 + e] = stat[e]
            for j in (4, 3, 5, 2, 6, 1, 7):
                rp_copy(h, j).start()
        for h in range(2):
            m = m_of[h]
            for j in range(1, 8):
                rp_copy(h, j).wait_recv()

            def total(k):
                return qb[h, m, k] + sum(tb[h, j, k] for j in range(7))

            psq = jnp.sum(total(8), axis=1, keepdims=True)
            dsq = jnp.sum(total(9), axis=1, keepdims=True)
            ratio = jnp.sqrt((psq + epsilon) / (dsq + epsilon))
            old = wgt[h]
            weight = jnp.where(it > 0, jnp.sqrt(old * ratio), old)
            wgt[h] = weight
            pstep = step_scale / weight
            square = jnp.zeros((8, T), F32)
            for k in range(8):
                primal = pr[h, k]
                new = jnp.maximum(primal - pstep * (cost[k:k + 1, :] - total(k)), 0.0)
                change = new - primal
                square = square + change * change
                pr[h, k] = new
                xg[h][(g_of[h] * 8 + m) * 8 + k] = 2.0 * new - primal
            for j in range(1, 4):
                ca_copy(h, j).wait_send()
            dg[h][q * 10 + 8] = square
            for j in (4, 3, 5, 2, 6, 1, 7):
                ap_copy(h, j).start()
        for h in range(2):
            for j in range(1, 8):
                ap_copy(h, j, True).wait_recv()
            copies = az_copies(h)
            for i in range(4):
                copies[i].start()
        for h in range(2):
            back, copies = az_copies(h, True), az_copies(h)
            back[0].wait_recv()
            copies[4].start()
            back[1].wait_recv()
            copies[5].start()

        @pl.when(it == 0)
        def _():
            for l in range(1, LEAD_MAX + 1):
                lag_copy(l).wait_recv()
            for h in range(2):
                rows = slice(8 * h, 8 * h + 8)
                for k in range(8):
                    lanes = slice(k * T, (k + 1) * T)
                    periods = jnp.broadcast_to(lead[k:k + 1, :], (8, T))
                    lagged = jnp.zeros((8, T), F32)
                    for l in range(1, LEAD_MAX + 1):
                        lagged = jnp.where(periods == l, lag[l - 1, rows, lanes], lagged)
                    rhs[h, k] = dem[rows, lanes] - return_share * lagged
            for l in range(1, LEAD_MAX + 1):
                lag_copy(l).wait_send()

        for h in range(2):
            back = az_copies(h, True)
            for i in (2, 3, 4, 5):
                back[i].wait_recv()
            products(h, xg, (O_C0, O_C1)[h], O_PR, True)
            for r in range(RT):
                yb[h, r] = s_buf[tab[O_LR + r]]
            for j in (2, 1, 3):
                cs_copy(h, j).start()
        for h in range(2):
            for j in range(1, 4):
                cs_copy(h, j).wait_recv()
            dstep = step_scale * wgt[h]
            square = jnp.zeros((8, T), F32)
            for k in range(8):
                push = yb[h, q * 8 + k] + (cr[h, 0, k] + cr[h, 1, k] + cr[h, 2, k])
                old = dg[h][q * 10 + k]
                new = old + dstep * (rhs[h, k] - push)
                change = new - old
                square = square + change * change
                dg[h][q * 10 + k] = new
            dg[h][q * 10 + 9] = square

            @pl.when(it < ITERS - 1)
            def _():
                for j in (2, 1, 3):
                    ca_copy(h, j).start()

        for h in range(2):
            for copies in (rz_copies(h), az_copies(h)):
                for i in range(6):
                    copies[i].wait_send()
            for j in range(1, 8):
                rp_copy(h, j).wait_send()
                ap_copy(h, j).wait_send()
            for j in range(1, 4):
                cs_copy(h, j).wait_send()
        return carry

    lax.fori_loop(0, ITERS, iteration, 0)

    for h in range(2):
        for e in range(2):
            fs[0, 2 * h + e] = dg[h][q * 10 + 8 + e]

    def fi_group(stage):
        if stage == 0:
            return [(b, (q + j) % 4) for j in range(1, 4)], fc, 0
        if stage == 1:
            return [(band_of(0, (z + j) % 4, m_of[0]), q) for j in range(1, 4)], fz, 3
        return [(band_of(0, z, (m_of[0] + j) % 8), q) for j in range(1, 8)], fp, 6

    def fi_copies(stage):
        group, dst, at = fi_group(stage)
        return [
            rc(fs.at[stage], dst.at[i], fi_s.at[at + i], fi_r.at[at + i], *to) for i, to in enumerate(group)
        ]

    for stage in range(3):
        copies = fi_copies(stage)
        for c in copies:
            c.start()
        if stage == 0:
            for h in range(2):
                for k in range(8):
                    prim_out[8 * h:8 * h + 8, k * T:(k + 1) * T] = pr[h, k]
                    dual_out[8 * h:8 * h + 8, k * T:(k + 1) * T] = dg[h][q * 10 + k]
        for c in copies:
            c.wait_recv()
        dst = fi_group(stage)[1]
        fs[stage + 1] = fs[stage] + sum(dst[i] for i in range(len(copies)))
    for h in range(2):
        psq = jnp.sum(fs[3, 2 * h], axis=1, keepdims=True)
        dsq = jnp.sum(fs[3, 2 * h + 1], axis=1, keepdims=True)
        ratio = jnp.sqrt((psq + epsilon) / (dsq + epsilon))
        w_out[8 * h:8 * h + 8, :] = jnp.sqrt(wgt[h] * ratio)
    for stage in range(3):
        for c in fi_copies(stage):
            c.wait_send()


def on_device(
    demand, lead_periods, matrix_tiles, tile_pos, cost_vector, primal_init, dual_init, weight_init
):
    table = index_table(tile_pos)
    vmem = pl.BlockSpec(memory_space=pltpu.VMEM)
    dma = pltpu.SemaphoreType.DMA

    def buf(*shape, dtype=F32):
        return pltpu.VMEM(shape, dtype)

    primal, dual, weight = pl.pallas_call(
        kernel,
        out_shape=(
            jax.ShapeDtypeStruct((16, 1024), F32),
            jax.ShapeDtypeStruct((16, 1024), F32),
            jax.ShapeDtypeStruct((16, T), F32),
        ),
        in_specs=[
            pl.BlockSpec(memory_space=pltpu.SMEM), vmem, vmem, pl.BlockSpec(memory_space=pl.ANY),
            vmem, vmem, vmem, vmem,
        ],
        out_specs=(vmem, vmem, vmem),
        scratch_shapes=[
            buf(NT, T, T),
            buf(NT, 2, T, T, dtype=BF16),
            buf(NT + 1, 8, T),
            buf(CT, 8, T),
            buf(CT, 8, T),
            buf(2, 264, 8, T),
            buf(2, 2, 34, 8, T),
            buf(2, 2, 66, 8, T),
            buf(2, 8, 10, 8, T),
            buf(2, 7, 10, 8, T),
            buf(40, 8, T),
            buf(40, 8, T),
            buf(2, RT, 8, T),
            buf(2, 3, 8, 8, T),
            buf(2, 8, 8, T),
            buf(2, 8, 8, T),
            buf(4, 16, 1024),
            buf(2, 8, T),
            buf(4, 4, 8, T),
            buf(3, 4, 8, T),
            buf(3, 4, 8, T),
            buf(7, 4, 8, T),
            dma((CHUNKS,)), dma((4,)), dma((4,)),
            dma((2, 3)), dma((2, 3)), dma((2, 6)), dma((2, 6)), dma((2, 7)), dma((2, 7)),
            dma((2, 7)), dma((2, 7)), dma((2, 6)), dma((2, 6)), dma((2, 3)), dma((2, 3)),
            dma((13,)), dma((13,)),
        ],
        compiler_params=pltpu.CompilerParams(
            has_side_effects=True, vmem_limit_bytes=48 * 2**20
        ),
    )(
        table,
        demand.T,
        lead_periods.reshape(8, T),
        matrix_tiles.reshape(NT, T, T),
        cost_vector.reshape(8, T),
        primal_init.T,
        dual_init.T,
        jnp.broadcast_to(weight_init[:, None], (16, T)),
    )
    return primal.T, dual.T, weight[:, 0]


def solution(mesh):
    in_specs = (
        P(("band", "col"), None),
        P(("band", "col")),
        P("band", "col", None, None, None),
        P("band", "col", None),
        P(("band", "col")),
        P(("band", "col"), None),
        P(("band", "col"), None),
        P(),
    )
    out_specs = (P(("band", "col"), None), P(("band", "col"), None), P())
    return jax.shard_map(
        on_device, mesh=mesh, in_specs=in_specs, out_specs=out_specs, check_vma=False
    )
```

time: 1260 us -> 209 us (0.17)
  waiting for transfers between devices: 885 us -> 0 us
  blocking collectives: 227 us -> 0 us
  Pallas kernels: 0 us -> 199 us
  matrix products: 76.5 us -> 0 us
  other arithmetic: 26.2 us -> 1.93 us
  local copies, waits for them, and re-layouts: 23.4 us -> 6.49 us
  between operations: 14.4 us -> 0.7 us
    all_gather x3 -> x0, waiting for transfers between devices: 459 us -> none  [on_device(): lax.all_gather(2.0 * primal_new - primal, 'band', axis=0, tiled=True)]
    reduce_scatter x6 -> x0, waiting for transfers between devices: 398 us -> none  [the longest x3 285 us: on_device(): lax.psum_scatter(partial_value, 'band', scatter_dimension=0, tiled=True)]
    pallas_call x0 -> x1, Pallas kernels: none -> 199 us  [on_device(): pl.pallas_call(kernel, out_shape=(jax.ShapeDtypeStruct((16, 1024), F32),...]
    psum x3 -> x0, blocking collectives: 194 us -> none  [on_device(): dual_square = lax.psum(dual_local, ('band', 'col'))]
    dot_general x9 -> x0, matrix products: 76.5 us -> none  [the longest x3 46.1 us: forward_part(): jnp.einsum('tij,tjs->tis', matrix_tiles, picked, precision=highest)]
    all_gather x3 -> x0, blocking collectives: 32.7 us -> none  [on_device(): band_dual = lax.all_gather(dual_vars, 'col', axis=0, tiled=True)]
    ppermute x4 -> x0, waiting for transfers between devices: 28.5 us -> none  [passed_along(): return lax.ppermute(value, axis, pairs)]
    reshape x15 -> x0, local copies, waits for them, and re-layouts: 15.7 us -> none  [the longest x6 5.96 us: forward_part(): return result.reshape(units_row * tile_size, scen_count)]
  transfers between devices with their start and end apart: 13 -> 0, of which waited for: 13 -> 0; matrix products, arithmetic and copies ran while one was open for 0% -> 0% of each run, Pallas kernels for 0% -> 0%
where the time goes in v1:
time: 209 us; the launch traced here: 208 us
  Pallas kernels  199 us (95%)
  local copies, waits for them, and re-layouts  6.49 us (3%)
    pallas_call x1, Pallas kernels, on_device(): pl.pallas_call(kernel, out_shape=(jax.ShapeDtypeStruct((16, 1024), F32),...  199 us
    unnamed x12, local copies, waits for them, and re-layouts  5.14 us

profile of v1, /device:TPU:1, one launch (start us, length us, event | category | flops | bytes accessed | tf_op | source)
XLA Modules:
  0.0 207.7 jit_solution(10057781263628539675)
XLA Ops:
  0.6 0.7 broadcast_in_dim.92.w0
  1.4 0.7 constant_dynamic-update-slice_fusion.7
  2.0 0.1 select_reduce_fusion.2
  2.1 0.1 select_reduce_fusion.4
  2.2 0.7 constant_dynamic-update-slice_fusion.6
  3.0 0.1 select_reduce_fusion.3
  3.1 0.1 select_reduce_fusion
  3.2 0.1 select_reduce_fusion.1
  3.3 0.0 copy-start
  3.3 0.8 copy-done
  4.2 0.0 copy-start.1
  4.2 0.8 copy-done.1
  5.0 0.0 copy-start.2
  5.0 0.8 copy-done.2
  5.9 0.0 copy-start.3
  5.9 0.7 copy-done.3
  6.5 0.0 copy-start.4
  6.5 0.7 copy-done.4
  7.2 198.6 %shard_map.103 = (f32[16,1024]{1,0:T(8,128)S(1)}, f32[16,1024]{1,0:T(8,128)S(1)}, f32[16,128]{1,0:T(8,128)S(1)}) custom-call(s32[1184]{0:T(1024)S(1)} %constant_dynamic-update-slice_fusion.tab, f32[16,1024]{1,0:T(8,128)S(1)} %bitcast.25, s32[8,128]{1,0:T(8,128)S(1)} %bitcast.30, f32[128,128,128]{2,1,0:T(8,128)} %bitcast.32, f32[8,128]{1,0:T(8,128)S(1)} %bitcast.31, ...), custom_call_target="tpu_custom_call" | custom-call | tf_op jit(solution)/shard_map/pallas_call | solution.py:413
  205.8 0.6 slice_reduce_fusion
  206.5 0.6 copy.21
  207.1 0.6 copy.22
  (7 shorter events, 0.1 us)
Async XLA Ops:
  3.3 0.8 copy-start
  4.2 0.8 copy-start.1
  5.0 0.8 copy-start.2
  5.9 0.7 copy-start.3
  6.5 0.7 copy-start.4

commit v2 on v1

v2 whole, which is shorter than its diff:
```python
import jax
import jax.numpy as jnp
from jax import lax
from jax.experimental import pallas as pl
from jax.experimental.pallas import tpu as pltpu
from jax.sharding import PartitionSpec as P

ITERS = 3
LEAD_MAX = 4
step_scale = 0.45
return_share = 0.6
epsilon = 1e-06

NT = 128
T = 128
CT = 256
RT = 32
F32 = jnp.float32
BF16 = jnp.bfloat16
CHUNKS = 16
MESH = pl.DeviceIdType.MESH

O_ROW, O_C0, O_C1, O_PC, O_PR = 0, 128, 256, 384, 512
O_L0, O_L1, O_LR = 640, 896, 1152
TABLE = 1184


def index_table(pos):
    pos = pos.reshape(-1)
    t = jnp.arange(NT, dtype=jnp.int32)
    row, col = pos // CT, pos % CT

    def order(c):
        k, z, x, y = c % 8, (c // 8) % 4, (c // 32) % 2, c // 64
        chunk, kk = k // 4, k % 4
        return (((z * 2 + chunk) * 4 + y) * 2 + x) * 4 + kk, (((y * 2 + chunk) * 4 + z) * 2 + x) * 4 + kk

    def prev(key):
        same = (key[:, None] == key[None, :]) & (t[:, None] < t[None, :])
        found = jnp.max(jnp.where(same, t[:, None], -1), axis=0)
        return jnp.where(found < 0, NT, found)

    def last(key, count):
        ids = jnp.arange(count, dtype=jnp.int32)
        found = jnp.max(jnp.where(key[:, None] == ids[None, :], t[:, None], -1), axis=0)
        return jnp.where(found < 0, NT, found)

    c0, c1 = order(col)
    drow = (row // 8) * 10 + row % 8
    return jnp.concatenate(
        [drow, c0, c1, prev(col), prev(row), last(c0, CT), last(c1, CT), last(row, RT)]
    )


def split(v):
    hi = v.astype(BF16).astype(F32)
    return hi, v - hi


class Copies:
    def __init__(self, make):
        self.make = make

    def __getitem__(self, i):
        return self.make(i)


def kernel(
    tab, w0, dem_in, lead_in, a_hbm, cost_in, prim_in, dual_in,
    prim_out, dual_out, w_out,
    dem, lead, cost, prim0, dual0,
    af, wt, s0, s1, xg0, xg1, pb, fb, rb, qb, tb, dg0, dg1, yb, cr, pr, rhs, lag, wgt, fs, fa, fp,
    in_sem, a_sem, lag_s, lag_r, ca_s, ca_r, rz_s, rz_r, rp_s, rp_r, ap_s, ap_r, az_s, az_r, cs_s, cs_r,
    fi_s, fi_r,
):
    b = lax.axis_index("band")
    q = lax.axis_index("col")
    y, x, z = b // 8, (b // 4) % 2, b % 4
    xg, dg, s_buf = (xg0, xg1), (dg0, dg1), (s0, s1)
    both = range(2)

    def rc(src, dst, ss, rs, band, col):
        return pltpu.make_async_remote_copy(
            src_ref=src, dst_ref=dst, send_sem=ss, recv_sem=rs,
            device_id=(band, col), device_id_type=MESH,
        )

    g_of = (z, y)
    m_of = (y * 2 + x, z * 2 + x)

    def band_of(h, g, m):
        o, xx = m // 2, m % 2
        return o * 8 + xx * 4 + g if h == 0 else g * 8 + xx * 4 + o

    near = [
        (band_of(0, (z + i) % 4, m_of[0]), (q + j) % 4) for i in range(4) for j in range(4) if i or j
    ]
    plane = [(band_of(0, z, (m_of[0] + j) % 8), q) for j in range(1, 8)]

    def a_copy(i):
        n = NT // CHUNKS
        return pltpu.make_async_copy(a_hbm.at[pl.ds(i * n, n)], af.at[pl.ds(i * n, n)], a_sem.at[i])

    def lag_copy(l):
        return rc(dem, lag.at[l - 1], lag_s.at[l - 1], lag_r.at[l - 1], (b + l) % 32, q)

    def ca_copy(h, j):
        own = dg[h].at[pl.ds(q * 10, 10)]
        return rc(own, own, ca_s.at[h, j - 1], ca_r.at[h, j - 1], b, (q + j) % 4)

    def ca_recv(h, j):
        slot = dg[h].at[pl.ds(((q + 4 - j) % 4) * 10, 10)]
        return rc(slot, slot, ca_s.at[h, j - 1], ca_r.at[h, j - 1], b, (q + 4 - j) % 4)

    def ring(h):
        g = g_of[h]
        return g, (g + 1) % 4, (g + 3) % 4, (g + 2) % 4

    def half_of(c, half):
        return ((0, 18), (18, 16))[half] if c == 0 else ((34, 16), (50, 16))[half]

    def rz_copies(h, c):
        g, up, dn, opp = ring(h)
        m = m_of[h]
        bu, bd = band_of(h, up, m), band_of(h, dn, m)

        def piece(block, half):
            at, n = half_of(c, half)
            return pb.at[h, pl.ds(block * 66 + at, n)]

        def into(side, half):
            at, n = half_of(c, half)
            return rb.at[h, side, pl.ds(at, n)]

        def make(i):
            src, dst, to = (
                lambda: (piece(opp, 0), fb.at[h, c, 0, pl.ds(0, half_of(c, 0)[1])], bu),
                lambda: (piece(opp, 1), fb.at[h, c, 1, pl.ds(0, 16)], bd),
                lambda: (piece(up, 1), into(0, 1), bu),
                lambda: (piece(dn, 0), into(1, 0), bd),
                lambda: (piece(up, 0), into(0, 0), bu),
                lambda: (piece(dn, 1), into(1, 1), bd),
            )[i]()
            return rc(src, dst, rz_s.at[h, c, i], rz_r.at[h, c, i], to, q)

        return Copies(make)

    def rp_copy(h, c, j):
        m2 = (m_of[h] + j) % 8
        n = pl.ds(0, 4 if c else 6)
        return rc(
            qb.at[h, c, m2, n], tb.at[h, c, j - 1, n], rp_s.at[h, c, j - 1], rp_r.at[h, c, j - 1],
            band_of(h, g_of[h], m2), q,
        )

    def ap_copy(h, c, j, back=False):
        m = m_of[h]
        m2 = (m + 8 - j) % 8 if back else (m + j) % 8
        slot = xg[h].at[pl.ds(((g_of[h] * 2 + c) * 8 + (m2 if back else m)) * 4, 4)]
        return rc(slot, slot, ap_s.at[h, c, j - 1], ap_r.at[h, c, j - 1], band_of(h, g_of[h], m2), q)

    def az_copies(h, c, back=False):
        g, up, dn, opp = ring(h)
        m = m_of[h]
        bu, bd = band_of(h, up, m), band_of(h, dn, m)
        lo, hi = (dn, up) if back else (g, g)
        spec = (
            (lo, 0, bu), (hi, 1, bd), (lo, 1, bu), (hi, 0, bd),
            (opp if back else dn, 0, bu), (opp if back else up, 1, bd),
        )

        def make(i):
            block, half, to = spec[i]
            slot = xg[h].at[pl.ds((block * 2 + c) * 32 + half * 16, 16)]
            return rc(slot, slot, az_s.at[h, c, i], az_r.at[h, c, i], to, q)

        return Copies(make)

    def cs_copy(h, j):
        q2 = (q + j) % 4
        return rc(yb.at[h, pl.ds(q2 * 8, 8)], cr.at[h, j - 1], cs_s.at[h, j - 1], cs_r.at[h, j - 1], b, q2)

    inputs = [
        pltpu.make_async_copy(src, dst, in_sem.at[i])
        for i, (src, dst) in enumerate(
            ((dual_in, dual0), (dem_in, dem), (prim_in, prim0), (cost_in, cost), (lead_in, lead))
        )
    ]
    for c in inputs:
        c.start()
    for i in range(CHUNKS):
        a_copy(i).start()
    greeted = near + plane
    greeted = greeted + [(band_of(1, y, (m_of[1] + j) % 8), q) for j in range(1, 8)]
    greeted = greeted + [(band_of(1, (y + j) % 4, m_of[1]), q) for j in (1, 3)]
    greeted = greeted + [((b + l) % 32, q) for l in (1, 2, 3, 4, 28, 29, 30, 31)]
    barrier = pltpu.get_barrier_semaphore()
    for to in greeted:
        pl.semaphore_signal(barrier, inc=1, device_id=to, device_id_type=MESH)
    zero = jnp.zeros((8, T), F32)
    sublane = lax.broadcasted_iota(jnp.int32, (8, T), 0)
    lane = lax.broadcasted_iota(jnp.int32, (8, T), 1)
    for c in inputs:
        c.wait()
    for h in both:
        for k in range(8):
            dg[h][q * 10 + k] = dual0[8 * h:8 * h + 8, k * T:(k + 1) * T]
            pr[h, k] = prim0[8 * h:8 * h + 8, k * T:(k + 1) * T]
        dg[h][q * 10 + 8] = zero
        dg[h][q * 10 + 9] = zero
        weight = zero
        for i in range(8):
            weight = jnp.where(sublane == i, w0[8 * h + i], weight)
        wgt[h] = weight
        s_buf[h][NT] = zero
    pl.semaphore_wait(barrier, len(greeted))
    for h in both:
        for j in (2, 1, 3):
            ca_copy(h, j).start()
    for l in range(1, LEAD_MAX + 1):
        lag_copy(l).start()

    for i in range(CHUNKS):
        a_copy(i).wait()
        n = NT // CHUNKS

        def prep(t, carry):
            v = af[t]
            hi = v.astype(BF16)
            wt[t, 0] = hi
            wt[t, 1] = (v - hi.astype(F32)).astype(BF16)
            return carry

        lax.fori_loop(i * n, (i + 1) * n, prep, 0, unroll=2)

    def products(src, offsets, o_prev, forward):
        def pair(p, carry):
            ts = (2 * p, 2 * p + 1)
            rows = []
            for t in ts:
                for h in both:
                    rows += split(src[h][tab[offsets[h] + t]])
            lhs = jnp.concatenate(rows, axis=0).astype(BF16)
            lhs = jnp.concatenate([lhs, lhs], axis=1)
            (h1, l1), (h2, l2) = [(wt[t, 0], wt[t, 1]) for t in ts]
            if forward:
                quarters, contract = (h1, l1, h2, l2), 1
            else:
                quarters, contract = (h1, h2, l1, l2), 0
            w = jnp.concatenate(
                [jnp.concatenate(quarters[:2], axis=1), jnp.concatenate(quarters[2:], axis=1)], axis=0
            )
            out = lax.dot_general(lhs, w, (((1,), (contract,)), ((), ())), preferred_element_type=F32)
            for i, t in enumerate(ts):
                before = tab[o_prev + t]
                for h in both:
                    at, lanes = 32 * i + 16 * h, slice(i * T, (i + 1) * T)
                    s_buf[h][t] = out[at:at + 8, lanes] + out[at + 8:at + 16, lanes] + s_buf[h][before]
            return carry

        lax.fori_loop(0, NT // 2, pair, 0, unroll=8)

    def place(which, c, stat):
        blocks = [ring(h)[which] for h in both]
        if c == 0:
            for h in both:
                for e in range(2):
                    pb[h, blocks[h] * 66 + e] = stat[h][e]

        def one(i, carry):
            for h in both:
                last = tab[(O_L0, O_L1)[h] + blocks[h] * 64 + c * 32 + i]
                pb[h, blocks[h] * 66 + (34 if c else 2) + i] = s_buf[h][last]
            return carry

        lax.fori_loop(0, 32, one, 0, unroll=8)

    def start_ring(which, c, stat, copies):
        place(which, c, stat)
        for i in copies:
            for h in both:
                rz_copies(h, c)[i].start()

    def relay_ring(c):
        for h in both:
            g, up, dn, opp = ring(h)
            copies = rz_copies(h, c)
            at, n = half_of(c, 0)
            copies[0].wait_recv()
            here = pl.ds(up * 66 + at, n)
            pb[h, here] = pb[h, here] + fb[h, c, 0, 0:n]
            copies[4].start()
            at, n = half_of(c, 1)
            copies[1].wait_recv()
            here = pl.ds(dn * 66 + at, n)
            pb[h, here] = pb[h, here] + fb[h, c, 1, 0:n]
            copies[5].start()

    def start_plane(c):
        for h in both:
            copies = rz_copies(h, c)
            for i in (2, 3, 4, 5):
                copies[i].wait_recv()

            def ring_sum(i):
                return pb[h, g_of[h] * 66 + i] + rb[h, 0, i] + rb[h, 1, i]

            for m in range(8):
                for k in range(4):
                    qb[h, c, m, k] = ring_sum((34 if c else 2) + m * 4 + k)
            if c == 0:
                for e in range(2):
                    stat = ring_sum(e)
                    for m in range(8):
                        qb[h, c, m, 4 + e] = stat
            for j in (4, 3, 5, 2, 6, 1, 7):
                rp_copy(h, c, j).start()

    def new_weight(old, primal_square, dual_square):
        return jnp.sqrt(old * jnp.sqrt((primal_square + epsilon) / (dual_square + epsilon)))

    def update(c, it, squares):
        for h in both:
            m = m_of[h]
            for j in range(1, 8):
                rp_copy(h, c, j).wait_recv()

            def total(k):
                return qb[h, c, m, k] + sum(tb[h, c, j, k] for j in range(7))

            if c == 0:
                psq = jnp.sum(total(4), axis=1, keepdims=True)
                dsq = jnp.sum(total(5), axis=1, keepdims=True)
                old = wgt[h]
                wgt[h] = jnp.where(it > 0, new_weight(old, psq, dsq), old)
            pstep = step_scale / wgt[h]
            for kk in range(4):
                k = c * 4 + kk
                primal = pr[h, k]
                new = jnp.maximum(primal - pstep * (cost[k:k + 1, :] - total(kk)), 0.0)
                change = new - primal
                squares[h] = squares[h] + change * change
                pr[h, k] = new
                xg[h][((g_of[h] * 2 + c) * 8 + m) * 4 + kk] = 2.0 * new - primal
            for j in (4, 3, 5, 2, 6, 1, 7):
                ap_copy(h, c, j).start()

    def start_spread(c):
        for h in both:
            for j in range(1, 8):
                ap_copy(h, c, j, True).wait_recv()
            copies = az_copies(h, c)
            for i in range(4):
                copies[i].start()

    def relay_spread(c):
        for h in both:
            back, copies = az_copies(h, c, True), az_copies(h, c)
            back[0].wait_recv()
            copies[4].start()
            back[1].wait_recv()
            copies[5].start()

    def iteration(it, carry):
        for h in both:
            for j in range(1, 4):
                ca_recv(h, j).wait_recv()
        products(dg, (O_ROW, O_ROW), O_PC, False)
        stat = [[sum(dg[h][c * 10 + 8 + e] for c in range(4)) for e in range(2)] for h in both]
        start_ring(3, 0, stat, (0, 1))
        start_ring(1, 0, stat, (2,))
        start_ring(2, 0, stat, (3,))
        start_ring(0, 0, stat, ())
        place(3, 1, stat)
        relay_ring(0)
        for i in (0, 1):
            for h in both:
                rz_copies(h, 1)[i].start()
        start_ring(1, 1, stat, (2,))
        start_ring(2, 1, stat, (3,))
        start_ring(0, 1, stat, ())
        start_plane(0)
        relay_ring(1)
        start_plane(1)
        squares = [zero, zero]
        update(0, it, squares)
        update(1, it, squares)
        for h in both:
            for j in range(1, 4):
                ca_copy(h, j).wait_send()
            dg[h][q * 10 + 8] = squares[h]
        start_spread(0)
        relay_spread(0)
        start_spread(1)
        relay_spread(1)

        @pl.when(it == 0)
        def _():
            for l in range(1, LEAD_MAX + 1):
                lag_copy(l).wait_recv()
            for h in both:
                rows = slice(8 * h, 8 * h + 8)
                for k in range(8):
                    lanes = slice(k * T, (k + 1) * T)
                    periods = jnp.broadcast_to(lead[k:k + 1, :], (8, T))
                    lagged = jnp.zeros((8, T), F32)
                    for l in range(1, LEAD_MAX + 1):
                        lagged = jnp.where(periods == l, lag[l - 1, rows, lanes], lagged)
                    rhs[h, k] = dem[rows, lanes] - return_share * lagged
            for l in range(1, LEAD_MAX + 1):
                lag_copy(l).wait_send()

        for c in range(2):
            for h in both:
                back = az_copies(h, c, True)
                for i in (2, 3, 4, 5):
                    back[i].wait_recv()
        products(xg, (O_C0, O_C1), O_PR, True)
        for h in both:
            for r in range(RT):
                yb[h, r] = s_buf[h][tab[O_LR + r]]
            for j in (2, 1, 3):
                cs_copy(h, j).start()
        for h in both:
            for j in range(1, 4):
                cs_copy(h, j).wait_recv()
            dstep = step_scale * wgt[h]
            square = zero
            for k in range(8):
                push = yb[h, q * 8 + k] + (cr[h, 0, k] + cr[h, 1, k] + cr[h, 2, k])
                old = dg[h][q * 10 + k]
                new = old + dstep * (rhs[h, k] - push)
                change = new - old
                square = square + change * change
                dg[h][q * 10 + k] = new
            dg[h][q * 10 + 9] = square

            @pl.when(it < ITERS - 1)
            def _():
                for j in (2, 1, 3):
                    ca_copy(h, j).start()

        for h in both:
            for c in range(2):
                for copies in (rz_copies(h, c), az_copies(h, c)):
                    for i in range(6):
                        copies[i].wait_send()
                for j in range(1, 8):
                    rp_copy(h, c, j).wait_send()
                    ap_copy(h, c, j).wait_send()
            for j in range(1, 4):
                cs_copy(h, j).wait_send()
        return carry

    lax.fori_loop(0, ITERS, iteration, 0)

    packed = zero
    for h in both:
        for e in range(2):
            packed = jnp.where(
                lane == 2 * h + e, jnp.sum(dg[h][q * 10 + 8 + e], axis=1, keepdims=True), packed
            )
    fs[0] = packed
    for stage, (group, dst, at) in enumerate(((near, fa, 0), (plane, fp, 15))):
        copies = [
            rc(fs.at[stage], dst.at[i], fi_s.at[at + i], fi_r.at[at + i], *to) for i, to in enumerate(group)
        ]
        for c in copies:
            c.start()
        if stage == 0:
            for h in both:
                for k in range(8):
                    prim_out[8 * h:8 * h + 8, k * T:(k + 1) * T] = pr[h, k]
                    dual_out[8 * h:8 * h + 8, k * T:(k + 1) * T] = dg[h][q * 10 + k]
        for c in copies:
            c.wait_recv()
        fs[stage + 1] = fs[stage] + sum(dst[i] for i in range(len(copies)))
        for c in copies:
            c.wait_send()
    sums = fs[2]
    for h in both:
        psq, dsq = [
            jnp.sum(jnp.where(lane == 2 * h + e, sums, 0.0), axis=1, keepdims=True) for e in range(2)
        ]
        w_out[8 * h:8 * h + 8, :] = new_weight(wgt[h], psq, dsq)


def on_device(
    demand, lead_periods, matrix_tiles, tile_pos, cost_vector, primal_init, dual_init, weight_init
):
    table = index_table(tile_pos)
    vmem = pl.BlockSpec(memory_space=pltpu.VMEM)
    smem = pl.BlockSpec(memory_space=pltpu.SMEM)
    hbm = pl.BlockSpec(memory_space=pl.ANY)
    dma = pltpu.SemaphoreType.DMA

    def buf(*shape, dtype=F32):
        return pltpu.VMEM(shape, dtype)

    primal, dual, weight = pl.pallas_call(
        kernel,
        out_shape=(
            jax.ShapeDtypeStruct((16, 1024), F32),
            jax.ShapeDtypeStruct((16, 1024), F32),
            jax.ShapeDtypeStruct((16, T), F32),
        ),
        in_specs=[smem, smem] + [hbm] * 6,
        out_specs=(vmem, vmem, vmem),
        scratch_shapes=[
            buf(16, 1024),
            buf(8, T, dtype=jnp.int32),
            buf(8, T),
            buf(16, 1024),
            buf(16, 1024),
            buf(NT, T, T),
            buf(NT, 2, T, T, dtype=BF16),
            buf(NT + 1, 8, T),
            buf(NT + 1, 8, T),
            buf(CT, 8, T),
            buf(CT, 8, T),
            buf(2, 264, 8, T),
            buf(2, 2, 2, 18, 8, T),
            buf(2, 2, 66, 8, T),
            buf(2, 2, 8, 6, 8, T),
            buf(2, 2, 7, 6, 8, T),
            buf(40, 8, T),
            buf(40, 8, T),
            buf(2, RT, 8, T),
            buf(2, 3, 8, 8, T),
            buf(2, 8, 8, T),
            buf(2, 8, 8, T),
            buf(4, 16, 1024),
            buf(2, 8, T),
            buf(3, 8, T),
            buf(15, 8, T),
            buf(7, 8, T),
            dma((5,)), dma((CHUNKS,)), dma((4,)), dma((4,)),
            dma((2, 3)), dma((2, 3)), dma((2, 2, 6)), dma((2, 2, 6)), dma((2, 2, 7)), dma((2, 2, 7)),
            dma((2, 2, 7)), dma((2, 2, 7)), dma((2, 2, 6)), dma((2, 2, 6)), dma((2, 3)), dma((2, 3)),
            dma((22,)), dma((22,)),
        ],
        compiler_params=pltpu.CompilerParams(
            collective_id=0, has_side_effects=True, vmem_limit_bytes=60 * 2**20
        ),
    )(
        table,
        weight_init,
        demand.T,
        lead_periods.reshape(8, T),
        matrix_tiles.reshape(NT, T, T),
        cost_vector.reshape(8, T),
        primal_init.T,
        dual_init.T,
    )
    return primal.T, dual.T, weight[:, 0]


def solution(mesh):
    in_specs = (
        P(("band", "col"), None),
        P(("band", "col")),
        P("band", "col", None, None, None),
        P("band", "col", None),
        P(("band", "col")),
        P(("band", "col"), None),
        P(("band", "col"), None),
        P(),
    )
    out_specs = (P(("band", "col"), None), P(("band", "col"), None), P())
    return jax.shard_map(
        on_device, mesh=mesh, in_specs=in_specs, out_specs=out_specs, check_vma=False
    )
```

time: 209 us -> 184 us (0.88)
  Pallas kernels: 199 us -> 176 us
    pallas_call x1, Pallas kernels: 199 us -> 176 us  [on_device(): pl.pallas_call(kernel, out_shape=(jax.ShapeDtypeStruct((16, 1024), F32),...]
    unnamed x12 -> x4, local copies, waits for them, and re-layouts: 5.14 us -> 3.54 us
where the time goes in v2:
time: 184 us; the launch traced here: 183 us
  Pallas kernels  176 us (96%)
  local copies, waits for them, and re-layouts  4.86 us (3%)
  other arithmetic  1.93 us (1%)
    pallas_call x1, Pallas kernels, on_device(): pl.pallas_call(kernel, out_shape=(jax.ShapeDtypeStruct((16, 1024), F32),...  176 us

profile of v2, /device:TPU:1, one launch (start us, length us, event | category | flops | bytes accessed | tf_op | source)
XLA Modules:
  0.0 183.4 jit_solution(17954660408415404054)
XLA Ops:
  0.6 0.7 constant_dynamic-update-slice_fusion.7
  1.3 0.1 select_reduce_fusion.2
  1.4 0.1 select_reduce_fusion.4
  1.5 0.7 constant_dynamic-update-slice_fusion.6
  2.2 0.1 select_reduce_fusion.3
  2.4 0.1 select_reduce_fusion
  2.5 0.1 select_reduce_fusion.1
  2.6 0.0 copy-start
  2.6 0.6 copy-done
  3.2 175.9 %shard_map.103 = (f32[16,1024]{1,0:T(8,128)}, f32[16,1024]{1,0:T(8,128)}, f32[16,128]{1,0:T(8,128)}) custom-call(s32[1184]{0:T(1024)} %copy-done, f32[16]{0:T(128)} %w0.1, f32[16,1024]{1,0:T(8,128)} %bitcast.26, s32[8,128]{1,0:T(8,128)} %bitcast.31, f32[128,128,128]{2,1,0:T(8,128)} %bitcast.25, f32[8,128]{1,0:T(8,128)} %bitcast.32, f32[16,1024]{1,0:T(8,128)} %bitcast.27, ...), custom_call_target="tpu_custom_call" | custom-call | tf_op jit(solution)/shard_map/pallas_call | solution.py:500
  179.2 1.3 slice_reduce_fusion
  180.5 1.5 copy.21
  182.0 1.5 copy.22
  (7 shorter events, 0.1 us)
Async XLA Ops:
  2.6 0.6 copy-start

commit v3 on v2

v3 whole, which is shorter than its diff:
```python
import jax
import jax.numpy as jnp
from jax import lax
from jax.experimental import pallas as pl
from jax.experimental.pallas import tpu as pltpu
from jax.sharding import PartitionSpec as P

ITERS = 3
LEAD_MAX = 4
step_scale = 0.45
return_share = 0.6
epsilon = 1e-06

NT = 128
T = 128
CT = 256
RT = 32
F32 = jnp.float32
BF16 = jnp.bfloat16
CHUNKS = 16
MESH = pl.DeviceIdType.MESH

O_ROW, O_C, O_PC, O_PR, O_LC, O_LR = 0, 128, 256, 384, 512, 768


def index_table(pos):
    pos = pos.reshape(-1)
    t = jnp.arange(NT, dtype=jnp.int32)
    row, col = pos // CT, pos % CT

    def order(c):
        k, z, x, y = c % 8, (c // 8) % 4, (c // 32) % 2, c // 64
        kk = k % 4
        return jnp.where(k < 4, ((z * 4 + y) * 2 + x) * 4 + kk, 128 + ((y * 4 + z) * 2 + x) * 4 + kk)

    def prev(key):
        same = (key[:, None] == key[None, :]) & (t[:, None] < t[None, :])
        found = jnp.max(jnp.where(same, t[:, None], -1), axis=0)
        return jnp.where(found < 0, NT, found)

    def last(key, count):
        ids = jnp.arange(count, dtype=jnp.int32)
        found = jnp.max(jnp.where(key[:, None] == ids[None, :], t[:, None], -1), axis=0)
        return jnp.where(found < 0, NT, found)

    drow = (row // 8) % 2 * 17 + row // 16 * 8 + row % 8
    return jnp.concatenate(
        [drow, order(col), prev(col), prev(row), last(order(col), CT), last(row, RT)]
    )


def split(v):
    hi = v.astype(BF16).astype(F32)
    return hi, v - hi


def kernel(
    tab, w0, dem_in, lead_in, a_hbm, cost_in, prim_in, dual_in,
    prim_out, dual_out, w_out,
    dem, lead, cost, prim0, dual0,
    af, wt, s0, s1, xg0, xg1, pb, rb, qb, tb, dg0, dg1, yb, yc, ych, yx, pr, rhs, lag, wgt, fs, fc, fa,
    in_sem, a_sem, lag_s, lag_r, ca_s, ca_r, rz_s, rz_r, rp_s, rp_r, ap_s, ap_r, az_s, az_r, col_s, col_r,
    sums_r, rh_s, rh_r, fi_s, fi_r,
):
    b = lax.axis_index("band")
    q = lax.axis_index("col")
    y, x, z = b // 8, (b // 4) % 2, b % 4
    xg, dg, s_buf = (xg0, xg1), (dg0, dg1), (s0, s1)
    both = range(2)

    def rc(src, dst, ss, rs, band, col):
        return pltpu.make_async_remote_copy(
            src_ref=src, dst_ref=dst, send_sem=ss, recv_sem=rs,
            device_id=(band, col), device_id_type=MESH,
        )

    g_of = (z, y)
    m_of = (y * 2 + x, z * 2 + x)

    def band_of(c, g, m):
        o, xx = m // 2, m % 2
        return o * 8 + xx * 4 + g if c == 0 else g * 8 + xx * 4 + o

    band = [((b + i) % 32, q) for i in range(1, 32)]
    core, chip = q % 2, q // 2
    other_core, other_chip = q + 1 - 2 * core, (q + 2) % 4

    def a_copy(i):
        n = NT // CHUNKS
        return pltpu.make_async_copy(a_hbm.at[pl.ds(i * n, n)], af.at[pl.ds(i * n, n)], a_sem.at[i])

    def lag_copy(l):
        return rc(dem, lag.at[l - 1], lag_s.at[l - 1], lag_r.at[l - 1], (b + l) % 32, q)

    def ca_copy(h, j):
        own = dg[h].at[pl.ds(core * 17 + chip * 8, 8)]
        return rc(own, own, ca_s.at[h, j - 1], ca_r.at[h, j - 1], b, (q + j) % 4)

    def ca_recv(h, j):
        q2 = (q + 4 - j) % 4
        slot = dg[h].at[pl.ds(q2 % 2 * 17 + q2 // 2 * 8, 8)]
        return rc(slot, slot, ca_s.at[h, j - 1], ca_r.at[h, j - 1], b, q2)

    def terms_copy(h):
        return rc(yb.at[h, 1 - core], yc.at[h], col_s.at[0, h], col_r.at[0, h], b, other_core)

    def sums_copy(h, it):
        return rc(ych.at[h], yx.at[h, it], col_s.at[1, h], sums_r.at[h, it], b, other_chip)

    def prices_copy(h, back=False):
        slot = dg[h].at[pl.ds((1 - core if back else core) * 17, 17)]
        return rc(slot, slot, col_s.at[2, h], col_r.at[2, h], b, other_core)

    def rhs_copy(h, back=False):
        slot = rhs.at[h, pl.ds((1 - chip if back else chip) * 8, 8)]
        return rc(slot, slot, rh_s.at[h], rh_r.at[h], b, other_chip)

    def rz_copy(h, c, j):
        g2 = (g_of[c] + j) % 4
        part = pl.ds(1, 32) if c else pl.ds(0, 33)
        return rc(
            pb.at[h, c, g2, part], rb.at[h, c, j - 1, part], rz_s.at[h, c, j - 1], rz_r.at[h, c, j - 1],
            band_of(c, g2, m_of[c]), q,
        )

    def rp_copy(h, c, j):
        m2 = (m_of[c] + j) % 8
        part = pl.ds(1, 4) if c else pl.ds(0, 5)
        return rc(
            qb.at[h, c, m2, part], tb.at[h, c, j - 1, part], rp_s.at[h, c, j - 1], rp_r.at[h, c, j - 1],
            band_of(c, g_of[c], m2), q,
        )

    def ap_copy(h, c, j, back=False):
        m = m_of[c]
        m2 = (m + 8 - j) % 8 if back else (m + j) % 8
        slot = xg[h].at[pl.ds(c * 128 + g_of[c] * 32 + (m2 if back else m) * 4, 4)]
        return rc(slot, slot, ap_s.at[h, c, j - 1], ap_r.at[h, c, j - 1], band_of(c, g_of[c], m2), q)

    def az_copy(h, c, j, back=False):
        g = g_of[c]
        g2 = (g + 4 - j) % 4 if back else (g + j) % 4
        slot = xg[h].at[pl.ds(c * 128 + (g2 if back else g) * 32, 32)]
        return rc(slot, slot, az_s.at[h, c, j - 1], az_r.at[h, c, j - 1], band_of(c, g2, m_of[c]), q)

    inputs = [
        pltpu.make_async_copy(src, dst, in_sem.at[i])
        for i, (src, dst) in enumerate(
            ((dual_in, dual0), (dem_in, dem), (prim_in, prim0), (cost_in, cost), (lead_in, lead))
        )
    ]
    for c in inputs:
        c.start()
    for i in range(CHUNKS):
        a_copy(i).start()
    greeted = band + [(b, (q + j) % 4) for j in (1, 2, 3)]
    barrier = pltpu.get_barrier_semaphore()
    for to in greeted:
        pl.semaphore_signal(barrier, inc=1, device_id=to, device_id_type=MESH)
    zero = jnp.zeros((8, T), F32)
    sublane = lax.broadcasted_iota(jnp.int32, (8, T), 0)
    lane = lax.broadcasted_iota(jnp.int32, (8, T), 1)
    for c in inputs:
        c.wait()
    for h in both:
        for k in range(8):
            dg[h][core * 17 + chip * 8 + k] = dual0[8 * h:8 * h + 8, k * T:(k + 1) * T]
            pr[h, k] = prim0[8 * h:8 * h + 8, k * T:(k + 1) * T]
        dg[h][16] = zero
        dg[h][33] = zero
        weight = zero
        for i in range(8):
            weight = jnp.where(sublane == i, w0[8 * h + i], weight)
        wgt[h] = weight
        s_buf[h][NT] = zero

    def prep_chunks(first, end):
        n = NT // CHUNKS

        def prep(t, carry):
            v = af[t]
            hi = v.astype(BF16)
            wt[t, 0] = hi
            wt[t, 1] = (v - hi.astype(F32)).astype(BF16)
            return carry

        for i in range(first, end):
            a_copy(i).wait()
            lax.fori_loop(i * n, (i + 1) * n, prep, 0, unroll=2)

    prep_chunks(0, CHUNKS // 2)
    pl.semaphore_wait(barrier, len(greeted))
    for h in both:
        for j in (2, 1, 3):
            ca_copy(h, j).start()
    for l in range(1, LEAD_MAX + 1):
        lag_copy(l).start()
    prep_chunks(CHUNKS // 2, CHUNKS)

    def products(h, src, o_src, o_prev, forward):
        def pair(p, carry):
            ts = (2 * p, 2 * p + 1)
            rows = []
            for t in ts:
                rows += split(src[tab[o_src + t]])
            lhs = jnp.concatenate(rows, axis=0).astype(BF16)
            lhs = jnp.concatenate([lhs, lhs], axis=1)
            (h1, l1), (h2, l2) = [(wt[t, 0], wt[t, 1]) for t in ts]
            if forward:
                quarters, contract = (h1, l1, h2, l2), 1
            else:
                quarters, contract = (h1, h2, l1, l2), 0
            w = jnp.concatenate(
                [jnp.concatenate(quarters[:2], axis=1), jnp.concatenate(quarters[2:], axis=1)], axis=0
            )
            out = lax.dot_general(lhs, w, (((1,), (contract,)), ((), ())), preferred_element_type=F32)
            for i, t in enumerate(ts):
                at, lanes = 16 * i, slice(i * T, (i + 1) * T)
                s_buf[h][t] = out[at:at + 8, lanes] + out[at + 8:at + 16, lanes] + s_buf[h][tab[o_prev + t]]
            return carry

        lax.fori_loop(0, NT // 2, pair, 0, unroll=16)

    def place(h, c, g, stat):
        if c == 0:
            pb[h, c, g, 0] = stat

        def one(i, carry):
            pb[h, c, g, 1 + i] = s_buf[h][tab[O_LC + c * 128 + g * 32 + i]]
            return carry

        lax.fori_loop(0, 32, one, 0, unroll=16)

    def start_ring(h, stat):
        for j in (2, 1, 3, 0):
            for c in range(2):
                place(h, c, (g_of[c] + j) % 4, stat)
                if j:
                    rz_copy(h, c, j).start()

    def start_plane(h):
        for c in range(2):
            for j in (1, 3, 2):
                rz_copy(h, c, j).wait_recv()

            def ring_sum(i):
                return (pb[h, c, g_of[c], i] + rb[h, c, 0, i]) + (rb[h, c, 1, i] + rb[h, c, 2, i])

            for m in range(8):
                for k in range(4):
                    qb[h, c, m, 1 + k] = ring_sum(1 + m * 4 + k)
            if c == 0:
                stat = ring_sum(0)
                for m in range(8):
                    qb[h, c, m, 0] = stat
            for j in (4, 3, 5, 2, 6, 1, 7):
                rp_copy(h, c, j).start()

    def new_weight(old, sums, at):
        psq, dsq = [
            jnp.sum(jnp.where(lane == at + e, sums, 0.0), axis=1, keepdims=True) for e in range(2)
        ]
        return jnp.sqrt(old * jnp.sqrt((psq + epsilon) / (dsq + epsilon)))

    def lanes_sum(v):
        return jnp.sum(v, axis=1, keepdims=True)

    def update(h, it):
        square = zero
        for c in range(2):
            m = m_of[c]
            for j in range(1, 8):
                rp_copy(h, c, j).wait_recv()

            def total(k):
                return qb[h, c, m, k] + sum(tb[h, c, j, k] for j in range(7))

            if c == 0:
                old = wgt[h]
                wgt[h] = jnp.where(it > 0, new_weight(old, total(0), 0), old)
            pstep = step_scale / wgt[h]
            for kk in range(4):
                k = c * 4 + kk
                primal = pr[h, k]
                new = jnp.maximum(primal - pstep * (cost[k:k + 1, :] - total(1 + kk)), 0.0)
                change = new - primal
                square = square + change * change
                pr[h, k] = new
                xg[h][c * 128 + g_of[c] * 32 + m * 4 + kk] = 2.0 * new - primal
            for j in (4, 3, 5, 2, 6, 1, 7):
                ap_copy(h, c, j).start()
        yb[h, 1 - core, 16] = square
        yb[h, core, 16] = square

    def start_spread(h):
        for c in range(2):
            for j in range(1, 8):
                ap_copy(h, c, j, True).wait_recv()
            for j in (2, 1, 3):
                az_copy(h, c, j).start()

    def iteration(it, carry):
        for h in both:
            @pl.when(it == 0)
            def _():
                for j in range(1, 4):
                    ca_recv(h, j).wait_recv()

            @pl.when(it > 0)
            def _():
                prices_copy(h, True).wait_recv()

            products(h, dg[h], O_ROW, O_PC, False)
            start_ring(h, jnp.where(lane == 0, dg[h][16], dg[h][16] + dg[h][33]))
        for h in both:
            start_plane(h)
        for h in both:
            update(h, it)
        for h in both:
            start_spread(h)

        @pl.when(it == 0)
        def _():
            for l in range(1, LEAD_MAX + 1):
                lag_copy(l).wait_recv()
            for h in both:
                rows = slice(8 * h, 8 * h + 8)
                for k in range(8):
                    lanes = slice(k * T, (k + 1) * T)
                    periods = jnp.broadcast_to(lead[k:k + 1, :], (8, T))
                    lagged = jnp.zeros((8, T), F32)
                    for l in range(1, LEAD_MAX + 1):
                        lagged = jnp.where(periods == l, lag[l - 1, rows, lanes], lagged)
                    rhs[h, chip * 8 + k] = dem[rows, lanes] - return_share * lagged
                rhs_copy(h).start()
            for l in range(1, LEAD_MAX + 1):
                lag_copy(l).wait_send()

        for h in both:
            for c in range(2):
                for j in (1, 3, 2):
                    az_copy(h, c, j, True).wait_recv()
            products(h, xg[h], O_C, O_PR, True)
            for r in range(RT):
                yb[h, r // 8 % 2, r // 16 * 8 + r % 8] = s_buf[h][tab[O_LR + r]]
            terms_copy(h).start()
        for h in both:
            terms_copy(h).wait_recv()
            ych[h] = yb[h, core] + yc[h]
            sums_copy(h, it).start()
        for h in both:
            @pl.when(it == 0)
            def _():
                rhs_copy(h, True).wait_recv()
                rhs_copy(h).wait_send()
                for j in range(1, 4):
                    ca_copy(h, j).wait_send()

            @pl.when(it > 0)
            def _():
                prices_copy(h).wait_send()

            sums_copy(h, it).wait_recv()
            dstep = step_scale * wgt[h]
            square = zero
            for k in range(16):
                push = ych[h, k] + yx[h, it, k]
                old = dg[h][core * 17 + k]
                new = old + dstep * (rhs[h, k] - push)
                change = new - old
                square = square + change * change
                dg[h][core * 17 + k] = new
            primal_square = lanes_sum(ych[h, 16] + yx[h, it, 16])
            dg[h][core * 17 + 16] = jnp.where(
                lane == 0, primal_square, jnp.where(lane == 1, lanes_sum(square), 0.0)
            )

            @pl.when(it < ITERS - 1)
            def _():
                prices_copy(h).start()

        for h in both:
            for c in range(2):
                for j in range(1, 4):
                    rz_copy(h, c, j).wait_send()
                    az_copy(h, c, j).wait_send()
                for j in range(1, 8):
                    rp_copy(h, c, j).wait_send()
                    ap_copy(h, c, j).wait_send()
            terms_copy(h).wait_send()
            sums_copy(h, it).wait_send()
        return carry

    lax.fori_loop(0, ITERS, iteration, 0)

    packed = zero
    for h in both:
        stat = dg[h][core * 17 + 16]
        for e in range(2):
            value = lanes_sum(jnp.where(lane == e, stat, 0.0))
            packed = jnp.where(lane == 2 * h + e, value, packed)
    fs[0] = packed
    first = rc(fs.at[0], fc, fi_s.at[31], fi_r.at[31], b, other_core)
    first.start()
    for h in both:
        for k in range(8):
            prim_out[8 * h:8 * h + 8, k * T:(k + 1) * T] = pr[h, k]
            dual_out[8 * h:8 * h + 8, k * T:(k + 1) * T] = dg[h][core * 17 + chip * 8 + k]
    first.wait_recv()
    fs[1] = jnp.where(lane % 2 == 0, packed, packed + fc[...])
    copies = [rc(fs.at[1], fa.at[i], fi_s.at[i], fi_r.at[i], *to) for i, to in enumerate(band)]
    for c in copies:
        c.start()
    for c in copies:
        c.wait_recv()
    sums = fs[1] + jnp.sum(fa[...], axis=0)
    for h in both:
        w_out[8 * h:8 * h + 8, :] = new_weight(wgt[h], sums, 2 * h)
    first.wait_send()
    for c in copies:
        c.wait_send()


def on_device(
    demand, lead_periods, matrix_tiles, tile_pos, cost_vector, primal_init, dual_init, weight_init
):
    table = index_table(tile_pos)
    vmem = pl.BlockSpec(memory_space=pltpu.VMEM)
    smem = pl.BlockSpec(memory_space=pltpu.SMEM)
    hbm = pl.BlockSpec(memory_space=pl.ANY)
    dma = pltpu.SemaphoreType.DMA

    def buf(*shape, dtype=F32):
        return pltpu.VMEM(shape, dtype)

    primal, dual, weight = pl.pallas_call(
        kernel,
        out_shape=(
            jax.ShapeDtypeStruct((16, 1024), F32),
            jax.ShapeDtypeStruct((16, 1024), F32),
            jax.ShapeDtypeStruct((16, T), F32),
        ),
        in_specs=[smem, smem] + [hbm] * 6,
        out_specs=(vmem, vmem, vmem),
        scratch_shapes=[
            buf(16, 1024),
            buf(8, T, dtype=jnp.int32),
            buf(8, T),
            buf(16, 1024),
            buf(16, 1024),
            buf(NT, T, T),
            buf(NT, 2, T, T, dtype=BF16),
            buf(NT + 1, 8, T),
            buf(NT + 1, 8, T),
            buf(CT, 8, T),
            buf(CT, 8, T),
            buf(2, 2, 4, 33, 8, T),
            buf(2, 2, 3, 33, 8, T),
            buf(2, 2, 8, 5, 8, T),
            buf(2, 2, 7, 5, 8, T),
            buf(34, 8, T),
            buf(34, 8, T),
            buf(2, 2, 17, 8, T),
            buf(2, 17, 8, T),
            buf(2, 17, 8, T),
            buf(2, ITERS, 17, 8, T),
            buf(2, 8, 8, T),
            buf(2, 16, 8, T),
            buf(4, 16, 1024),
            buf(2, 8, T),
            buf(2, 8, T),
            buf(8, T),
            buf(31, 8, T),
            dma((5,)), dma((CHUNKS,)), dma((4,)), dma((4,)),
            dma((2, 3)), dma((2, 3)), dma((2, 2, 3)), dma((2, 2, 3)), dma((2, 2, 7)), dma((2, 2, 7)),
            dma((2, 2, 7)), dma((2, 2, 7)), dma((2, 2, 3)), dma((2, 2, 3)), dma((3, 2)), dma((3, 2)),
            dma((2, ITERS)), dma((2,)), dma((2,)), dma((32,)), dma((32,)),
        ],
        compiler_params=pltpu.CompilerParams(
            collective_id=0, has_side_effects=True, vmem_limit_bytes=60 * 2**20
        ),
    )(
        table,
        weight_init,
        demand.T,
        lead_periods.reshape(8, T),
        matrix_tiles.reshape(NT, T, T),
        cost_vector.reshape(8, T),
        primal_init.T,
        dual_init.T,
    )
    return primal.T, dual.T, weight[:, 0]


def solution(mesh):
    in_specs = (
        P(("band", "col"), None),
        P(("band", "col")),
        P("band", "col", None, None, None),
        P("band", "col", None),
        P(("band", "col")),
        P(("band", "col"), None),
        P(("band", "col"), None),
        P(),
    )
    out_specs = (P(("band", "col"), None), P(("band", "col"), None), P())
    return jax.shard_map(
        on_device, mesh=mesh, in_specs=in_specs, out_specs=out_specs, check_vma=False
    )
```

time: 184 us -> 173 us (0.940)
  Pallas kernels: 176 us -> 165 us
    pallas_call x1, Pallas kernels: 176 us -> 165 us  [on_device(): pl.pallas_call(kernel, out_shape=(jax.ShapeDtypeStruct((16, 1024), F32),...]
where the time goes in v3:
time: 173 us; the launch traced here: 172 us
  Pallas kernels  165 us (95%)
  local copies, waits for them, and re-layouts  4.86 us (3%)
  other arithmetic  1.82 us (1%)
    pallas_call x1, Pallas kernels, on_device(): pl.pallas_call(kernel, out_shape=(jax.ShapeDtypeStruct((16, 1024), F32),...  165 us
    unnamed x4, local copies, waits for them, and re-layouts  3.53 us

profile of v3, /device:TPU:1, one launch (start us, length us, event | category | flops | bytes accessed | tf_op | source)
XLA Modules:
  0.0 172.5 jit_solution(15079033231368004623)
XLA Ops:
  0.6 0.7 constant_dynamic-update-slice_fusion.5
  1.3 0.1 select_reduce_fusion.1
  1.4 0.1 select_reduce_fusion.3
  1.5 0.7 constant_dynamic-update-slice_fusion.4
  2.2 0.1 select_reduce_fusion.2
  2.4 0.1 select_reduce_fusion
  2.5 0.0 copy-start
  2.5 0.6 copy-done
  3.1 165.1 %shard_map.103 = (f32[16,1024]{1,0:T(8,128)}, f32[16,1024]{1,0:T(8,128)}, f32[16,128]{1,0:T(8,128)}) custom-call(s32[800]{0:T(1024)} %copy-done, f32[16]{0:T(128)} %w0.1, f32[16,1024]{1,0:T(8,128)} %bitcast.26, s32[8,128]{1,0:T(8,128)} %bitcast.31, f32[128,128,128]{2,1,0:T(8,128)} %bitcast.25, f32[8,128]{1,0:T(8,128)} %bitcast.32, f32[16,1024]{1,0:T(8,128)} %bitcast.27, ...), custom_call_target="tpu_custom_call" | custom-call | tf_op jit(solution)/shard_map/pallas_call | solution.py:436
  168.2 1.3 slice_reduce_fusion
  169.6 1.5 copy.19
  171.0 1.5 copy.20
  (5 shorter events, 0.0 us)
Async XLA Ops:
  2.5 0.6 copy-start

commit v4 on v3

--- a/solution.py
+++ b/solution.py
@@ -58,7 +58,7 @@
     tab, w0, dem_in, lead_in, a_hbm, cost_in, prim_in, dual_in,
     prim_out, dual_out, w_out,
     dem, lead, cost, prim0, dual0,
-    af, wt, s0, s1, xg0, xg1, pb, rb, qb, tb, dg0, dg1, yb, yc, ych, yx, pr, rhs, lag, wgt, fs, fc, fa,
+    af, wt, s0, s1, xg0, xg1, pb, fb, rb, qb, tb, dg0, dg1, yb, yc, ych, yx, pr, rhs, lag, wgt, fs, fc, fa,
     in_sem, a_sem, lag_s, lag_r, ca_s, ca_r, rz_s, rz_r, rp_s, rp_r, ap_s, ap_r, az_s, az_r, col_s, col_r,
     sums_r, rh_s, rh_r, fi_s, fi_r,
 ):
@@ -115,12 +115,21 @@
         slot = rhs.at[h, pl.ds((1 - chip if back else chip) * 8, 8)]
         return rc(slot, slot, rh_s.at[h], rh_r.at[h], b, other_chip)
 
-    def rz_copy(h, c, j):
-        g2 = (g_of[c] + j) % 4
-        part = pl.ds(1, 32) if c else pl.ds(0, 33)
+    def ring(c):
+        g = g_of[c]
+        return g, (g + 1) % 4, (g + 3) % 4, (g + 2) % 4
+
+    def half_of(c, half):
+        return (17, 16) if half else (c, 17 - c)
+
+    def rz_copy(h, c, i):
+        g, up, dn, opp = ring(c)
+        block, side, half = ((opp, 0, 0), (opp, 1, 1), (up, 0, 1), (dn, 1, 0), (up, 0, 0), (dn, 1, 1))[i]
+        at, n = half_of(c, half)
+        src = pb.at[h, c, block, pl.ds(at, n)]
+        dst = fb.at[h, c, side, pl.ds(0, n)] if i < 2 else rb.at[h, c, side, pl.ds(at, n)]
         return rc(
-            pb.at[h, c, g2, part], rb.at[h, c, j - 1, part], rz_s.at[h, c, j - 1], rz_r.at[h, c, j - 1],
-            band_of(c, g2, m_of[c]), q,
+            src, dst, rz_s.at[h, c, i], rz_r.at[h, c, i], band_of(c, dn if side else up, m_of[c]), q
         )
 
     def rp_copy(h, c, j):
@@ -137,11 +146,15 @@
         slot = xg[h].at[pl.ds(c * 128 + g_of[c] * 32 + (m2 if back else m) * 4, 4)]
         return rc(slot, slot, ap_s.at[h, c, j - 1], ap_r.at[h, c, j - 1], band_of(c, g_of[c], m2), q)
 
-    def az_copy(h, c, j, back=False):
-        g = g_of[c]
-        g2 = (g + 4 - j) % 4 if back else (g + j) % 4
-        slot = xg[h].at[pl.ds(c * 128 + (g2 if back else g) * 32, 32)]
-        return rc(slot, slot, az_s.at[h, c, j - 1], az_r.at[h, c, j - 1], band_of(c, g2, m_of[c]), q)
+    def az_copy(h, c, i, back=False):
+        g, up, dn, opp = ring(c)
+        lo, hi = (dn, up) if back else (g, g)
+        block, half = (
+            (lo, 0), (hi, 1), (lo, 1), (hi, 0), (opp if back else dn, 0), (opp if back else up, 1)
+        )[i]
+        slot = xg[h].at[pl.ds(c * 128 + block * 32 + half * 16, 16)]
+        to = band_of(c, dn if i % 2 else up, m_of[c])
+        return rc(slot, slot, az_s.at[h, c, i], az_r.at[h, c, i], to, q)
 
     inputs = [
         pltpu.make_async_copy(src, dst, in_sem.at[i])
@@ -232,19 +245,29 @@
         lax.fori_loop(0, 32, one, 0, unroll=16)
 
     def start_ring(h, stat):
-        for j in (2, 1, 3, 0):
+        for which, copies in ((3, (0, 1)), (1, (2,)), (2, (3,)), (0, ())):
             for c in range(2):
-                place(h, c, (g_of[c] + j) % 4, stat)
-                if j:
-                    rz_copy(h, c, j).start()
+                place(h, c, ring(c)[which], stat)
+                for i in copies:
+                    rz_copy(h, c, i).start()
+
+    def relay_ring(h):
+        for c in range(2):
+            g, up, dn, opp = ring(c)
+            for side, block in ((0, up), (1, dn)):
+                rz_copy(h, c, side).wait_recv()
+                at, n = half_of(c, side)
+                here = pl.ds(at, n)
+                pb[h, c, block, here] = pb[h, c, block, here] + fb[h, c, side, 0:n]
+                rz_copy(h, c, 4 + side).start()
 
     def start_plane(h):
         for c in range(2):
-            for j in (1, 3, 2):
-                rz_copy(h, c, j).wait_recv()
+            for i in (2, 3, 4, 5):
+                rz_copy(h, c, i).wait_recv()
 
             def ring_sum(i):
-                return (pb[h, c, g_of[c], i] + rb[h, c, 0, i]) + (rb[h, c, 1, i] + rb[h, c, 2, i])
+                return pb[h, c, g_of[c], i] + rb[h, c, 0, i] + rb[h, c, 1, i]
 
             for m in range(8):
                 for k in range(4):
@@ -296,8 +319,14 @@
         for c in range(2):
             for j in range(1, 8):
                 ap_copy(h, c, j, True).wait_recv()
-            for j in (2, 1, 3):
-                az_copy(h, c, j).start()
+            for i in range(4):
+                az_copy(h, c, i).start()
+
+    def relay_spread(h):
+        for c in range(2):
+            for i in range(2):
+                az_copy(h, c, i, True).wait_recv()
+                az_copy(h, c, 4 + i).start()
 
     def iteration(it, carry):
         for h in both:
@@ -313,11 +342,15 @@
             products(h, dg[h], O_ROW, O_PC, False)
             start_ring(h, jnp.where(lane == 0, dg[h][16], dg[h][16] + dg[h][33]))
         for h in both:
+            relay_ring(h)
+        for h in both:
             start_plane(h)
         for h in both:
             update(h, it)
         for h in both:
             start_spread(h)
+        for h in both:
+            relay_spread(h)
 
         @pl.when(it == 0)
         def _():
@@ -338,8 +371,8 @@
 
         for h in both:
             for c in range(2):
-                for j in (1, 3, 2):
-                    az_copy(h, c, j, True).wait_recv()
+                for i in (2, 3, 4, 5):
+                    az_copy(h, c, i, True).wait_recv()
             products(h, xg[h], O_C, O_PR, True)
             for r in range(RT):
                 yb[h, r // 8 % 2, r // 16 * 8 + r % 8] = s_buf[h][tab[O_LR + r]]
@@ -381,9 +414,9 @@
 
         for h in both:
             for c in range(2):
-                for j in range(1, 4):
-                    rz_copy(h, c, j).wait_send()
-                    az_copy(h, c, j).wait_send()
+                for i in range(6):
+                    rz_copy(h, c, i).wait_send()
+                    az_copy(h, c, i).wait_send()
                 for j in range(1, 8):
                     rp_copy(h, c, j).wait_send()
                     ap_copy(h, c, j).wait_send()
@@ -455,7 +488,8 @@
             buf(CT, 8, T),
             buf(CT, 8, T),
             buf(2, 2, 4, 33, 8, T),
-            buf(2, 2, 3, 33, 8, T),
+            buf(2, 2, 2, 17, 8, T),
+            buf(2, 2, 2, 33, 8, T),
             buf(2, 2, 8, 5, 8, T),
             buf(2, 2, 7, 5, 8, T),
             buf(34, 8, T),
@@ -472,8 +506,8 @@
             buf(8, T),
             buf(31, 8, T),
             dma((5,)), dma((CHUNKS,)), dma((4,)), dma((4,)),
-            dma((2, 3)), dma((2, 3)), dma((2, 2, 3)), dma((2, 2, 3)), dma((2, 2, 7)), dma((2, 2, 7)),
-            dma((2, 2, 7)), dma((2, 2, 7)), dma((2, 2, 3)), dma((2, 2, 3)), dma((3, 2)), dma((3, 2)),
+            dma((2, 3)), dma((2, 3)), dma((2, 2, 6)), dma((2, 2, 6)), dma((2, 2, 7)), dma((2, 2, 7)),
+            dma((2, 2, 7)), dma((2, 2, 7)), dma((2, 2, 6)), dma((2, 2, 6)), dma((3, 2)), dma((3, 2)),
             dma((2, ITERS)), dma((2,)), dma((2,)), dma((32,)), dma((32,)),
         ],
         compiler_params=pltpu.CompilerParams(

time: 173 us -> 167 us (0.965)
  Pallas kernels: 165 us -> 160 us
    pallas_call x1, Pallas kernels: 165 us -> 160 us  [on_device(): pl.pallas_call(kernel, out_shape=(jax.ShapeDtypeStruct((16, 1024), F32),...]
where the time goes in v4:
time: 167 us
  Pallas kernels  160 us (96%)
  local copies, waits for them, and re-layouts  4.86 us (3%)
  other arithmetic  1.82 us (1%)
    pallas_call x1, Pallas kernels, on_device(): pl.pallas_call(kernel, out_shape=(jax.ShapeDtypeStruct((16, 1024), F32),...  160 us
    unnamed x4, local copies, waits for them, and re-layouts  3.53 us

profile of v4, /device:TPU:1, one launch (start us, length us, event | category | flops | bytes accessed | tf_op | source)
XLA Modules:
  0.0 167.1 jit_solution(13638956710630812521)
XLA Ops:
  0.6 0.7 constant_dynamic-update-slice_fusion.5
  1.3 0.1 select_reduce_fusion.1
  1.4 0.1 select_reduce_fusion.3
  1.5 0.7 constant_dynamic-update-slice_fusion.4
  2.2 0.1 select_reduce_fusion.2
  2.4 0.1 select_reduce_fusion
  2.5 0.0 copy-start
  2.5 0.6 copy-done
  3.1 159.7 %shard_map.103 = (f32[16,1024]{1,0:T(8,128)}, f32[16,1024]{1,0:T(8,128)}, f32[16,128]{1,0:T(8,128)}) custom-call(s32[800]{0:T(1024)} %copy-done, f32[16]{0:T(128)} %w0.1, f32[16,1024]{1,0:T(8,128)} %bitcast.26, s32[8,128]{1,0:T(8,128)} %bitcast.31, f32[128,128,128]{2,1,0:T(8,128)} %bitcast.25, f32[8,128]{1,0:T(8,128)} %bitcast.32, f32[16,1024]{1,0:T(8,128)} %bitcast.27, ...), custom_call_target="tpu_custom_call" | custom-call | tf_op jit(solution)/shard_map/pallas_call | solution.py:469
  162.8 1.3 slice_reduce_fusion
  164.1 1.5 copy.19
  165.6 1.5 copy.20
  (5 shorter events, 0.0 us)
Async XLA Ops:
  2.5 0.6 copy-start

commit v5 on v4

--- a/solution.py
+++ b/solution.py
@@ -210,7 +210,7 @@
         lag_copy(l).start()
     prep_chunks(CHUNKS // 2, CHUNKS)
 
-    def products(h, src, o_src, o_prev, forward):
+    def products(h, src, o_src, o_prev, forward, between=None, at=48):
         def pair(p, carry):
             ts = (2 * p, 2 * p + 1)
             rows = []
@@ -228,11 +228,14 @@
             )
             out = lax.dot_general(lhs, w, (((1,), (contract,)), ((), ())), preferred_element_type=F32)
             for i, t in enumerate(ts):
-                at, lanes = 16 * i, slice(i * T, (i + 1) * T)
-                s_buf[h][t] = out[at:at + 8, lanes] + out[at + 8:at + 16, lanes] + s_buf[h][tab[o_prev + t]]
+                row, lanes = 16 * i, slice(i * T, (i + 1) * T)
+                s_buf[h][t] = out[row:row + 8, lanes] + out[row + 8:row + 16, lanes] + s_buf[h][tab[o_prev + t]]
             return carry
 
-        lax.fori_loop(0, NT // 2, pair, 0, unroll=16)
+        lax.fori_loop(0, at, pair, 0, unroll=16)
+        if between:
+            between()
+        lax.fori_loop(at, NT // 2, pair, 0, unroll=16)
 
     def place(h, c, g, stat):
         if c == 0:
@@ -328,19 +331,53 @@
                 az_copy(h, c, i, True).wait_recv()
                 az_copy(h, c, 4 + i).start()
 
+    def transposed(h, between=None):
+        products(h, dg[h], O_ROW, O_PC, False, between)
+        start_ring(h, jnp.where(lane == 0, dg[h][16], dg[h][16] + dg[h][33]))
+
+    def send_sums(h, it):
+        terms_copy(h).wait_recv()
+        ych[h] = yb[h, core] + yc[h]
+        sums_copy(h, it).start()
+
+    def dual_update(h, it):
+        @pl.when(it == 0)
+        def _():
+            rhs_copy(h, True).wait_recv()
+            rhs_copy(h).wait_send()
+            for j in range(1, 4):
+                ca_copy(h, j).wait_send()
+
+        @pl.when(it > 0)
+        def _():
+            prices_copy(h).wait_send()
+
+        sums_copy(h, it).wait_recv()
+        dstep = step_scale * wgt[h]
+        square = zero
+        for k in range(16):
+            push = ych[h, k] + yx[h, it, k]
+            old = dg[h][core * 17 + k]
+            new = old + dstep * (rhs[h, k] - push)
+            change = new - old
+            square = square + change * change
+            dg[h][core * 17 + k] = new
+        primal_square = lanes_sum(ych[h, 16] + yx[h, it, 16])
+        dg[h][core * 17 + 16] = jnp.where(
+            lane == 0, primal_square, jnp.where(lane == 1, lanes_sum(square), 0.0)
+        )
+
     def iteration(it, carry):
-        for h in both:
-            @pl.when(it == 0)
-            def _():
-                for j in range(1, 4):
-                    ca_recv(h, j).wait_recv()
-
-            @pl.when(it > 0)
-            def _():
-                prices_copy(h, True).wait_recv()
-
-            products(h, dg[h], O_ROW, O_PC, False)
-            start_ring(h, jnp.where(lane == 0, dg[h][16], dg[h][16] + dg[h][33]))
+        @pl.when(it == 0)
+        def _():
+            for j in range(1, 4):
+                ca_recv(1, j).wait_recv()
+
+        @pl.when(it > 0)
+        def _():
+            prices_copy(1, True).wait_recv()
+
+        transposed(1)
         for h in both:
             relay_ring(h)
         for h in both:
@@ -373,45 +410,11 @@
             for c in range(2):
                 for i in (2, 3, 4, 5):
                     az_copy(h, c, i, True).wait_recv()
-            products(h, xg[h], O_C, O_PR, True)
+            products(h, xg[h], O_C, O_PR, True, (lambda: send_sums(0, it)) if h else None)
             for r in range(RT):
                 yb[h, r // 8 % 2, r // 16 * 8 + r % 8] = s_buf[h][tab[O_LR + r]]
             terms_copy(h).start()
-        for h in both:
-            terms_copy(h).wait_recv()
-            ych[h] = yb[h, core] + yc[h]
-            sums_copy(h, it).start()
-        for h in both:
-            @pl.when(it == 0)
-            def _():
-                rhs_copy(h, True).wait_recv()
-                rhs_copy(h).wait_send()
-                for j in range(1, 4):
-                    ca_copy(h, j).wait_send()
-
-            @pl.when(it > 0)
-            def _():
-                prices_copy(h).wait_send()
-
-            sums_copy(h, it).wait_recv()
-            dstep = step_scale * wgt[h]
-            square = zero
-            for k in range(16):
-                push = ych[h, k] + yx[h, it, k]
-                old = dg[h][core * 17 + k]
-                new = old + dstep * (rhs[h, k] - push)
-                change = new - old
-                square = square + change * change
-                dg[h][core * 17 + k] = new
-            primal_square = lanes_sum(ych[h, 16] + yx[h, it, 16])
-            dg[h][core * 17 + 16] = jnp.where(
-                lane == 0, primal_square, jnp.where(lane == 1, lanes_sum(square), 0.0)
-            )
-
-            @pl.when(it < ITERS - 1)
-            def _():
-                prices_copy(h).start()
-
+        send_sums(1, it)
         for h in both:
             for c in range(2):
                 for i in range(6):
@@ -421,9 +424,30 @@
                     rp_copy(h, c, j).wait_send()
                     ap_copy(h, c, j).wait_send()
             terms_copy(h).wait_send()
+        dual_update(0, it)
+
+        @pl.when(it < ITERS - 1)
+        def _():
+            prices_copy(0).start()
+            prices_copy(0, True).wait_recv()
+
+            def other_half():
+                dual_update(1, it)
+                prices_copy(1).start()
+
+            transposed(0, other_half)
+
+        @pl.when(it == ITERS - 1)
+        def _():
+            dual_update(1, it)
+
+        for h in both:
             sums_copy(h, it).wait_send()
         return carry
 
+    for j in range(1, 4):
+        ca_recv(0, j).wait_recv()
+    transposed(0)
     lax.fori_loop(0, ITERS, iteration, 0)
 
     packed = zero

time: 167 us -> 163 us (0.976)
  Pallas kernels: 160 us -> 155 us
    pallas_call x1, Pallas kernels: 160 us -> 155 us  [on_device(): pl.pallas_call(kernel, out_shape=(jax.ShapeDtypeStruct((16, 1024), F32),...]
where the time goes in v5:
time: 163 us
  Pallas kernels  155 us (95%)
  local copies, waits for them, and re-layouts  4.86 us (3%)
  other arithmetic  1.82 us (1%)
    pallas_call x1, Pallas kernels, on_device(): pl.pallas_call(kernel, out_shape=(jax.ShapeDtypeStruct((16, 1024), F32),...  155 us
    unnamed x4, local copies, waits for them, and re-layouts  3.53 us

profile of v5, /device:TPU:1, one launch (start us, length us, event | category | flops | bytes accessed | tf_op | source)
XLA Modules:
  0.0 162.5 jit_solution(2008102998171274462)
XLA Ops:
  0.6 0.7 constant_dynamic-update-slice_fusion.5
  1.3 0.1 select_reduce_fusion.1
  1.4 0.1 select_reduce_fusion.3
  1.5 0.7 constant_dynamic-update-slice_fusion.4
  2.2 0.1 select_reduce_fusion.2
  2.4 0.1 select_reduce_fusion
  2.5 0.0 copy-start
  2.5 0.6 copy-done
  3.1 155.1 %shard_map.103 = (f32[16,1024]{1,0:T(8,128)}, f32[16,1024]{1,0:T(8,128)}, f32[16,128]{1,0:T(8,128)}) custom-call(s32[800]{0:T(1024)} %copy-done, f32[16]{0:T(128)} %w0.1, f32[16,1024]{1,0:T(8,128)} %bitcast.26, s32[8,128]{1,0:T(8,128)} %bitcast.31, f32[128,128,128]{2,1,0:T(8,128)} %bitcast.25, f32[8,128]{1,0:T(8,128)} %bitcast.32, f32[16,1024]{1,0:T(8,128)} %bitcast.27, ...), custom_call_target="tpu_custom_call" | custom-call | tf_op jit(solution)/shard_map/pallas_call | solution.py:493
  158.2 1.3 slice_reduce_fusion
  159.6 1.5 copy.19
  161.0 1.5 copy.20
  (5 shorter events, 0.0 us)
Async XLA Ops:
  2.5 0.6 copy-start

commit v6 on v5

--- a/solution.py
+++ b/solution.py
@@ -20,33 +20,45 @@
 CHUNKS = 16
 MESH = pl.DeviceIdType.MESH
 
-O_ROW, O_C, O_PC, O_PR, O_LC, O_LR = 0, 128, 256, 384, 512, 768
+ROW, COL, PREV_COL, PREV_ROW, LAST_COL, LAST_ROW = 0, 1, 2, 3, 4, 6
 
 
 def index_table(pos):
-    pos = pos.reshape(-1)
-    t = jnp.arange(NT, dtype=jnp.int32)
-    row, col = pos // CT, pos % CT
-
-    def order(c):
-        k, z, x, y = c % 8, (c // 8) % 4, (c // 32) % 2, c // 64
-        kk = k % 4
-        return jnp.where(k < 4, ((z * 4 + y) * 2 + x) * 4 + kk, 128 + ((y * 4 + z) * 2 + x) * 4 + kk)
-
-    def prev(key):
-        same = (key[:, None] == key[None, :]) & (t[:, None] < t[None, :])
-        found = jnp.max(jnp.where(same, t[:, None], -1), axis=0)
+    shift = lax.shift_right_logical
+    here = jnp.broadcast_to(pos, (NT, NT))
+    above = here.T
+    u = lax.broadcasted_iota(jnp.int32, (NT, NT), 0)
+    t = lax.broadcasted_iota(jnp.int32, (NT, NT), 1)
+
+    def row(v):
+        return shift(v, 8)
+
+    def col(v):
+        return v & 255
+
+    def row_place(v):
+        r = row(v)
+        return (shift(r, 3) & 1) * 17 + shift(r, 4) * 8 + (r & 7)
+
+    def col_place(v):
+        k, z, x, y = v & 7, shift(v, 3) & 3, shift(v, 5) & 1, shift(col(v), 6)
+        kk = k & 3
+        return jnp.where(k < 4, z * 32 + y * 8 + x * 4 + kk, 128 + y * 32 + z * 8 + x * 4 + kk)
+
+    def latest(where):
+        found = jnp.max(jnp.where(where, u, -1), axis=0, keepdims=True)
         return jnp.where(found < 0, NT, found)
 
-    def last(key, count):
-        ids = jnp.arange(count, dtype=jnp.int32)
-        found = jnp.max(jnp.where(key[:, None] == ids[None, :], t[:, None], -1), axis=0)
-        return jnp.where(found < 0, NT, found)
-
-    drow = (row // 8) % 2 * 17 + row // 16 * 8 + row % 8
-    return jnp.concatenate(
-        [drow, order(col), prev(col), prev(row), last(order(col), CT), last(row, RT)]
-    )
+    place = col_place(above)
+    return [
+        row_place(pos),
+        col_place(pos),
+        latest((col(above) == col(here)) & (u < t)),
+        latest((row(above) == row(here)) & (u < t)),
+        latest(place == t),
+        latest(place == t + NT),
+        latest(row(above) == t),
+    ]
 
 
 def split(v):
@@ -55,10 +67,10 @@
 
 
 def kernel(
-    tab, w0, dem_in, lead_in, a_hbm, cost_in, prim_in, dual_in,
+    w0, pos_in, dem_in, lead_in, a_hbm, cost_in, prim_in, dual_in,
     prim_out, dual_out, w_out,
-    dem, lead, cost, prim0, dual0,
-    af, wt, s0, s1, xg0, xg1, pb, fb, rb, qb, tb, dg0, dg1, yb, yc, ych, yx, pr, rhs, lag, wgt, fs, fc, fa,
+    tab, tab_v, pos, dem, lead, cost, prim0, dual0,
+    af, wt, wf, s0, s1, xg0, xg1, pb, fb, rb, qb, tb, dg0, dg1, yb, yc, ych, yx, pr, rhs, lag, wgt, fs, fc, fa,
     in_sem, a_sem, lag_s, lag_r, ca_s, ca_r, rz_s, rz_r, rp_s, rp_r, ap_s, ap_r, az_s, az_r, col_s, col_r,
     sums_r, rh_s, rh_r, fi_s, fi_r,
 ):
@@ -159,7 +171,7 @@
     inputs = [
         pltpu.make_async_copy(src, dst, in_sem.at[i])
         for i, (src, dst) in enumerate(
-            ((dual_in, dual0), (dem_in, dem), (prim_in, prim0), (cost_in, cost), (lead_in, lead))
+            ((pos_in, pos), (dual_in, dual0), (dem_in, dem), (prim_in, prim0), (cost_in, cost), (lead_in, lead))
         )
     ]
     for c in inputs:
@@ -187,6 +199,12 @@
         wgt[h] = weight
         s_buf[h][NT] = zero
 
+    tab_v[...] = jnp.zeros((8, NT), jnp.int32)
+    for i, entry in enumerate(index_table(pos[...])):
+        tab_v[i:i + 1, :] = entry
+    table = pltpu.make_async_copy(tab_v, tab, in_sem.at[6])
+    table.start()
+
     def prep_chunks(first, end):
         n = NT // CHUNKS
 
@@ -202,6 +220,7 @@
             lax.fori_loop(i * n, (i + 1) * n, prep, 0, unroll=2)
 
     prep_chunks(0, CHUNKS // 2)
+    table.wait()
     pl.semaphore_wait(barrier, len(greeted))
     for h in both:
         for j in (2, 1, 3):
@@ -215,21 +234,18 @@
             ts = (2 * p, 2 * p + 1)
             rows = []
             for t in ts:
-                rows += split(src[tab[o_src + t]])
+                rows += split(src[tab[o_src, t]])
             lhs = jnp.concatenate(rows, axis=0).astype(BF16)
             lhs = jnp.concatenate([lhs, lhs], axis=1)
-            (h1, l1), (h2, l2) = [(wt[t, 0], wt[t, 1]) for t in ts]
-            if forward:
-                quarters, contract = (h1, l1, h2, l2), 1
-            else:
-                quarters, contract = (h1, h2, l1, l2), 0
+            tiles = wf if forward else wt
+            (h1, l1), (h2, l2) = [(tiles[t, 0], tiles[t, 1]) for t in ts]
             w = jnp.concatenate(
-                [jnp.concatenate(quarters[:2], axis=1), jnp.concatenate(quarters[2:], axis=1)], axis=0
+                [jnp.concatenate([h1, h2], axis=1), jnp.concatenate([l1, l2], axis=1)], axis=0
             )
-            out = lax.dot_general(lhs, w, (((1,), (contract,)), ((), ())), preferred_element_type=F32)
+            out = lax.dot_general(lhs, w, (((1,), (0,)), ((), ())), preferred_element_type=F32)
             for i, t in enumerate(ts):
                 row, lanes = 16 * i, slice(i * T, (i + 1) * T)
-                s_buf[h][t] = out[row:row + 8, lanes] + out[row + 8:row + 16, lanes] + s_buf[h][tab[o_prev + t]]
+                s_buf[h][t] = out[row:row + 8, lanes] + out[row + 8:row + 16, lanes] + s_buf[h][tab[o_prev, t]]
             return carry
 
         lax.fori_loop(0, at, pair, 0, unroll=16)
@@ -242,7 +258,7 @@
             pb[h, c, g, 0] = stat
 
         def one(i, carry):
-            pb[h, c, g, 1 + i] = s_buf[h][tab[O_LC + c * 128 + g * 32 + i]]
+            pb[h, c, g, 1 + i] = s_buf[h][tab[LAST_COL + c, g * 32 + i]]
             return carry
 
         lax.fori_loop(0, 32, one, 0, unroll=16)
@@ -332,7 +348,7 @@
                 az_copy(h, c, 4 + i).start()
 
     def transposed(h, between=None):
-        products(h, dg[h], O_ROW, O_PC, False, between)
+        products(h, dg[h], ROW, PREV_COL, False, between)
         start_ring(h, jnp.where(lane == 0, dg[h][16], dg[h][16] + dg[h][33]))
 
     def send_sums(h, it):
@@ -367,6 +383,18 @@
             lane == 0, primal_square, jnp.where(lane == 1, lanes_sum(square), 0.0)
         )
 
+    def turn(t, carry):
+        v = af[t].T
+        hi = v.astype(BF16)
+        wf[t, 0] = hi
+        wf[t, 1] = (v - hi.astype(F32)).astype(BF16)
+        return carry
+
+    def turn_some(it, first, end):
+        @pl.when(it == 0)
+        def _():
+            lax.fori_loop(first, end, turn, 0, unroll=2)
+
     def iteration(it, carry):
         @pl.when(it == 0)
         def _():
@@ -380,10 +408,14 @@
         transposed(1)
         for h in both:
             relay_ring(h)
+
+        turn_some(it, 0, 40)
         for h in both:
             start_plane(h)
+        turn_some(it, 40, 88)
         for h in both:
             update(h, it)
+        turn_some(it, 88, NT)
         for h in both:
             start_spread(h)
         for h in both:
@@ -410,9 +442,9 @@
             for c in range(2):
                 for i in (2, 3, 4, 5):
                     az_copy(h, c, i, True).wait_recv()
-            products(h, xg[h], O_C, O_PR, True, (lambda: send_sums(0, it)) if h else None)
+            products(h, xg[h], COL, PREV_ROW, True, (lambda: send_sums(0, it)) if h else None)
             for r in range(RT):
-                yb[h, r // 8 % 2, r // 16 * 8 + r % 8] = s_buf[h][tab[O_LR + r]]
+                yb[h, r // 8 % 2, r // 16 * 8 + r % 8] = s_buf[h][tab[LAST_ROW, r]]
             terms_copy(h).start()
         send_sums(1, it)
         for h in both:
@@ -481,7 +513,6 @@
 def on_device(
     demand, lead_periods, matrix_tiles, tile_pos, cost_vector, primal_init, dual_init, weight_init
 ):
-    table = index_table(tile_pos)
     vmem = pl.BlockSpec(memory_space=pltpu.VMEM)
     smem = pl.BlockSpec(memory_space=pltpu.SMEM)
     hbm = pl.BlockSpec(memory_space=pl.ANY)
@@ -497,15 +528,19 @@
             jax.ShapeDtypeStruct((16, 1024), F32),
             jax.ShapeDtypeStruct((16, T), F32),
         ),
-        in_specs=[smem, smem] + [hbm] * 6,
+        in_specs=[smem] + [hbm] * 7,
         out_specs=(vmem, vmem, vmem),
         scratch_shapes=[
+            pltpu.SMEM((8, NT), jnp.int32),
+            buf(8, NT, dtype=jnp.int32),
+            buf(1, NT, dtype=jnp.int32),
             buf(16, 1024),
             buf(8, T, dtype=jnp.int32),
             buf(8, T),
             buf(16, 1024),
             buf(16, 1024),
             buf(NT, T, T),
+            buf(NT, 2, T, T, dtype=BF16),
             buf(NT, 2, T, T, dtype=BF16),
             buf(NT + 1, 8, T),
             buf(NT + 1, 8, T),
@@ -529,7 +564,7 @@
             buf(2, 8, T),
             buf(8, T),
             buf(31, 8, T),
-            dma((5,)), dma((CHUNKS,)), dma((4,)), dma((4,)),
+            dma((7,)), dma((CHUNKS,)), dma((4,)), dma((4,)),
             dma((2, 3)), dma((2, 3)), dma((2, 2, 6)), dma((2, 2, 6)), dma((2, 2, 7)), dma((2, 2, 7)),
             dma((2, 2, 7)), dma((2, 2, 7)), dma((2, 2, 6)), dma((2, 2, 6)), dma((3, 2)), dma((3, 2)),
             dma((2, ITERS)), dma((2,)), dma((2,)), dma((32,)), dma((32,)),
@@ -538,8 +573,8 @@
             collective_id=0, has_side_effects=True, vmem_limit_bytes=60 * 2**20
         ),
     )(
-        table,
         weight_init,
+        tile_pos.reshape(1, NT),
         demand.T,
         lead_periods.reshape(8, T),
         matrix_tiles.reshape(NT, T, T),

time: 163 us -> 157 us (0.963)
  Pallas kernels: 155 us -> 152 us
  other arithmetic: 1.82 us -> 0 us
    pallas_call x1, Pallas kernels: 155 us -> 152 us  [on_device(): pl.pallas_call(kernel, out_shape=(jax.ShapeDtypeStruct((16, 1024), F32),...]
    unnamed x4 -> x2, local copies, waits for them, and re-layouts: 3.53 us -> 2.95 us
where the time goes in v6:
time: 157 us
  Pallas kernels  152 us (97%)
  local copies, waits for them, and re-layouts  4.27 us (3%)
    pallas_call x1, Pallas kernels, on_device(): pl.pallas_call(kernel, out_shape=(jax.ShapeDtypeStruct((16, 1024), F32),...  152 us

profile of v6, /device:TPU:1, one launch (start us, length us, event | category | flops | bytes accessed | tf_op | source)
XLA Modules:
  0.0 157.1 jit_solution(433234592412589255)
XLA Ops:
  0.6 152.2 %shard_map.103 = (f32[16,1024]{1,0:T(8,128)}, f32[16,1024]{1,0:T(8,128)}, f32[16,128]{1,0:T(8,128)}) custom-call(f32[16]{0:T(128)} %w0.1, s32[1,128]{1,0:T(1,128)} %bitcast.17, f32[16,1024]{1,0:T(8,128)} %bitcast.10, s32[8,128]{1,0:T(8,128)} %bitcast.15, f32[128,128,128]{2,1,0:T(8,128)} %bitcast.9, f32[8,128]{1,0:T(8,128)} %bitcast.16, f32[16,1024]{1,0:T(8,128)} %bitcast.11, ...), custom_call_target="tpu_custom_call" | custom-call | tf_op jit(solution)/shard_map/pallas_call | solution.py:524
  152.8 1.3 slice_reduce_fusion
  154.1 1.5 copy.13
  155.6 1.5 copy.14

commit v7 on v6

--- a/solution.py
+++ b/solution.py
@@ -248,10 +248,12 @@
                 s_buf[h][t] = out[row:row + 8, lanes] + out[row + 8:row + 16, lanes] + s_buf[h][tab[o_prev, t]]
             return carry
 
-        lax.fori_loop(0, at, pair, 0, unroll=16)
         if between:
+            lax.fori_loop(0, at, pair, 0, unroll=16)
             between()
-        lax.fori_loop(at, NT // 2, pair, 0, unroll=16)
+            lax.fori_loop(at, NT // 2, pair, 0, unroll=16)
+        else:
+            lax.fori_loop(0, NT // 2, pair, 0, unroll=32)
 
     def place(h, c, g, stat):
         if c == 0:

time: 157 us -> 156 us (level)
  no operation moved by 1% of the time
where the time goes in v7:
time: 156 us
  Pallas kernels  151 us (97%)
  local copies, waits for them, and re-layouts  4.27 us (3%)
    pallas_call x1, Pallas kernels, on_device(): pl.pallas_call(kernel, out_shape=(jax.ShapeDtypeStruct((16, 1024), F32),...  151 us

profile of v7, /device:TPU:1, one launch (start us, length us, event | category | flops | bytes accessed | tf_op | source)
XLA Modules:
  0.0 155.9 jit_solution(17764086891712700649)
XLA Ops:
  0.6 151.0 %shard_map.103 = (f32[16,1024]{1,0:T(8,128)}, f32[16,1024]{1,0:T(8,128)}, f32[16,128]{1,0:T(8,128)}) custom-call(f32[16]{0:T(128)} %w0.1, s32[1,128]{1,0:T(1,128)} %bitcast.17, f32[16,1024]{1,0:T(8,128)} %bitcast.10, s32[8,128]{1,0:T(8,128)} %bitcast.15, f32[128,128,128]{2,1,0:T(8,128)} %bitcast.9, f32[8,128]{1,0:T(8,128)} %bitcast.16, f32[16,1024]{1,0:T(8,128)} %bitcast.11, ...), custom_call_target="tpu_custom_call" | custom-call | tf_op jit(solution)/shard_map/pallas_call | solution.py:526
  151.6 1.3 slice_reduce_fusion
  152.9 1.5 copy.13
  154.4 1.5 copy.14

commit v8 on v7

--- a/solution.py
+++ b/solution.py
@@ -225,8 +225,6 @@
     for h in both:
         for j in (2, 1, 3):
             ca_copy(h, j).start()
-    for l in range(1, LEAD_MAX + 1):
-        lag_copy(l).start()
     prep_chunks(CHUNKS // 2, CHUNKS)
 
     def products(h, src, o_src, o_prev, forward, between=None, at=48):
@@ -414,6 +412,11 @@
         turn_some(it, 0, 40)
         for h in both:
             start_plane(h)
+        @pl.when(it == 0)
+        def _():
+            for l in range(1, LEAD_MAX + 1):
+                lag_copy(l).start()
+
         turn_some(it, 40, 88)
         for h in both:
             update(h, it)

time: 156 us -> 160 us (1.026)
  Pallas kernels: 151 us -> 155 us
    pallas_call x1, Pallas kernels: 151 us -> 155 us  [on_device(): pl.pallas_call(kernel, out_shape=(jax.ShapeDtypeStruct((16, 1024), F32),...]
where the time goes in v8:
time: 160 us
  Pallas kernels  155 us (97%)
  local copies, waits for them, and re-layouts  4.27 us (3%)
    pallas_call x1, Pallas kernels, on_device(): pl.pallas_call(kernel, out_shape=(jax.ShapeDtypeStruct((16, 1024), F32),...  155 us

profile of v8, /device:TPU:1, one launch (start us, length us, event | category | flops | bytes accessed | tf_op | source)
XLA Modules:
  0.0 159.9 jit_solution(6668252498285312764)
XLA Ops:
  0.6 155.0 %shard_map.103 = (f32[16,1024]{1,0:T(8,128)}, f32[16,1024]{1,0:T(8,128)}, f32[16,128]{1,0:T(8,128)}) custom-call(f32[16]{0:T(128)} %w0.1, s32[1,128]{1,0:T(1,128)} %bitcast.17, f32[16,1024]{1,0:T(8,128)} %bitcast.10, s32[8,128]{1,0:T(8,128)} %bitcast.15, f32[128,128,128]{2,1,0:T(8,128)} %bitcast.9, f32[8,128]{1,0:T(8,128)} %bitcast.16, f32[16,1024]{1,0:T(8,128)} %bitcast.11, ...), custom_call_target="tpu_custom_call" | custom-call | tf_op jit(solution)/shard_map/pallas_call | solution.py:529
  155.6 1.3 slice_reduce_fusion
  156.9 1.5 copy.13
  158.4 1.5 copy.14
